TPU v7x, 256 devices: a whole 4x4x8 slice. The times are simulated.
256 devices in a mesh: quartet: 128 (over z, y, x), pert: 2 (over core).
Axes of the slice: x: 4, y: 4, z: 8, core: 2. Of those that a mesh axis runs over, the one named last changes fastest.
Arguments:
- integrals: bfloat16 [1024, 1024, 1024], P(('quartet', 'pert')), may hold values from -0.1875 to 0.1875
- quartets: int32 [1024, 4], P(('quartet', 'pert')), may hold values from 0 to 63, as said below
- density: bfloat16 [131072, 2048], P(('quartet', 'pert')), may hold values from -6 to 6
- orbitals: bfloat16 [2048, 256], replicated, may hold values from -0.125 to 0.125
Outputs:
- response: float32 [131072, 256], P(('quartet', 'pert'))
Inputs may be any that keep to these rules, and one draw needn't show every extreme that they name: `quartets`: rows 4 m to 4 m + 3 are the quartet blocks of one device. Within such a group the first blocks lie in four different quarters of the 64 shell blocks (quarter = block // 16), and so do the second blocks and the third blocks.
All inputs are finite; a program needn't handle non-finite values.
Results may differ from a plain program's by a relative error of at most 0.0029.
Values may be sent and summed in bfloat16 or wider, within the bound.
A program may use at most 256 MiB of HBM per device.

v0:
```python
import jax
import jax.numpy as jnp
from jax import lax
from jax.sharding import PartitionSpec as P

P_SIZE = 64
S = 32
NB = 64


def tile_roles(blocks):
    bra_one, bra_two, ket_one, ket_two = (
        blocks[..., 0],
        blocks[..., 1],
        blocks[..., 2],
        blocks[..., 3],
    )
    need_rows = jnp.stack([ket_one, bra_one, bra_two, bra_two, bra_one, bra_one], axis=-1)
    need_cols = jnp.stack([ket_two, bra_two, ket_two, ket_one, ket_two, ket_one], axis=-1)
    out_rows = jnp.stack([bra_one, ket_one, bra_one, bra_one, bra_two, bra_two], axis=-1)
    out_cols = jnp.stack([bra_two, ket_two, ket_one, ket_two, ket_one, ket_two], axis=-1)
    return (need_rows, need_cols, out_rows, out_cols)


def quarter_ranks(rows, quarter_span):
    quarter = rows // quarter_span
    positions = jnp.arange(rows.shape[1])
    earlier = positions[None, :] < positions[:, None]
    same_quarter = quarter[:, :, None] == quarter[:, None, :]
    slot_rank = jnp.sum(jnp.logical_and(same_quarter, earlier[None]), axis=-1)
    return (quarter, slot_rank)


def owner_lookup(
    rows, cols, quarter, slot_rank, global_first, unit_count, quarter_span, block_count
):
    device_count, tile_count = rows.shape
    unit_ids = jnp.arange(unit_count)
    global_start = global_first + unit_ids * quarter_span
    pert_ids = global_start // block_count
    quarter_ids = global_start % block_count // quarter_span
    slot_ids = jnp.arange(6)
    matched = jnp.logical_and(
        quarter[:, None, None, :] == quarter_ids[None, :, None, None],
        slot_rank[:, None, None, :] == slot_ids[None, None, :, None],
    )
    chosen = jnp.sum(jnp.where(matched, jnp.arange(tile_count)[None, None, None, :], 0), axis=-1)
    chosen = chosen.reshape(device_count, -1)
    picked_rows = jnp.take_along_axis(rows, chosen, axis=1).reshape(device_count, unit_count, 6)
    picked_cols = jnp.take_along_axis(cols, chosen, axis=1).reshape(device_count, unit_count, 6)
    local_block = pert_ids[None, :, None] * block_count + picked_rows - global_first
    return (local_block * block_count + picked_cols).reshape(-1)


def request_positions(
    rows_mine, rank_mine, pert_count, block_count, block_rows, quarter_span, capacity
):
    global_row = jnp.arange(pert_count)[None, :] * block_count + rows_mine[:, None]
    owner_dev = global_row // block_rows
    unit_slot = global_row % block_rows // quarter_span
    return owner_dev * capacity + unit_slot * 6 + rank_mine[:, None]


def digest(integral, density_tiles, block_side):
    area = block_side * block_side
    integral_four = integral.reshape(block_side, block_side, block_side, block_side)
    paired_ps = integral_four.transpose(0, 2, 1, 3).reshape(area, area)
    paired_pt = integral_four.transpose(0, 3, 1, 2).reshape(area, area)
    coulomb_bra = jnp.einsum(
        "xc,bc->xb", density_tiles[0], integral, preferred_element_type=jnp.float32
    )
    coulomb_ket = jnp.einsum(
        "xb,bc->xc", density_tiles[1], integral, preferred_element_type=jnp.float32
    )
    exchange_ik = jnp.einsum(
        "xc,bc->xb", density_tiles[2], paired_ps, preferred_element_type=jnp.float32
    )
    exchange_il = jnp.einsum(
        "xc,bc->xb", density_tiles[3], paired_pt, preferred_element_type=jnp.float32
    )
    exchange_jk = jnp.einsum(
        "xb,bc->xc", density_tiles[4], paired_pt, preferred_element_type=jnp.float32
    )
    exchange_jl = jnp.einsum(
        "xb,bc->xc", density_tiles[5], paired_ps, preferred_element_type=jnp.float32
    )
    return jnp.stack(
        [
            coulomb_bra,
            coulomb_ket,
            -0.5 * exchange_ik,
            -0.5 * exchange_il,
            -0.5 * exchange_jk,
            -0.5 * exchange_jl,
        ]
    )


def per_device(integrals, quartets, density, orbitals):
    quartet_size = lax.axis_size("quartet")
    pert_size = lax.axis_size("pert")
    devices = quartet_size * pert_size
    myself = lax.axis_index("quartet") * pert_size + lax.axis_index("pert")
    block_side = S
    block_count = NB
    pert_count = P_SIZE
    tile_area = block_side * block_side
    quarter_span = block_count // 4
    block_rows = density.shape[0] // block_side
    unit_count = block_rows // quarter_span
    capacity = 6 * unit_count
    global_first = myself * block_rows
    all_lists = lax.all_gather(quartets, ("quartet", "pert"), axis=0, tiled=True).reshape(
        devices, -1, 4
    )
    need_rows, need_cols, out_rows, out_cols = tile_roles(all_lists)
    need_rows = need_rows.reshape(devices, -1)
    need_cols = need_cols.reshape(devices, -1)
    out_rows = out_rows.reshape(devices, -1)
    out_cols = out_cols.reshape(devices, -1)
    need_quarter, need_rank = quarter_ranks(need_rows, quarter_span)
    out_quarter, out_rank = quarter_ranks(out_rows, quarter_span)
    local_tiles = density.reshape(block_rows, block_side, block_count, block_side).transpose(
        0, 2, 1, 3
    )
    local_tiles = local_tiles.reshape(block_rows * block_count, tile_area)
    chosen_tiles = owner_lookup(
        need_rows,
        need_cols,
        need_quarter,
        need_rank,
        global_first,
        unit_count,
        quarter_span,
        block_count,
    )
    outgoing = local_tiles[chosen_tiles].reshape(quartet_size, pert_size, capacity, tile_area)
    received = lax.all_to_all(
        lax.all_to_all(outgoing, "quartet", split_axis=0, concat_axis=0, tiled=True),
        "pert",
        split_axis=1,
        concat_axis=1,
        tiled=True,
    )
    incoming = received.reshape(devices * capacity, tile_area)
    wanted = request_positions(
        need_rows[myself],
        need_rank[myself],
        pert_count,
        block_count,
        block_rows,
        quarter_span,
        capacity,
    )
    fetched = incoming[wanted].reshape(integrals.shape[0], 6, pert_count, tile_area)
    pieces = [
        digest(integrals[position], fetched[position], block_side)
        for position in range(integrals.shape[0])
    ]
    fock_terms = jnp.stack(pieces).reshape(-1, tile_area)
    places = request_positions(
        out_rows[myself],
        out_rank[myself],
        pert_count,
        block_count,
        block_rows,
        quarter_span,
        capacity,
    )
    inverse = jnp.argsort(places.reshape(-1))
    leaving = fock_terms[inverse].reshape(quartet_size, pert_size, capacity, tile_area)
    landed = lax.all_to_all(
        lax.all_to_all(leaving, "quartet", split_axis=0, concat_axis=0, tiled=True),
        "pert",
        split_axis=1,
        concat_axis=1,
        tiled=True,
    )
    arrived = landed.reshape(devices * capacity, tile_area)
    targets = owner_lookup(
        out_rows,
        out_cols,
        out_quarter,
        out_rank,
        global_first,
        unit_count,
        quarter_span,
        block_count,
    )
    summed = jax.ops.segment_sum(arrived, targets, num_segments=block_rows * block_count)
    rounded = summed.astype(jnp.bfloat16).reshape(block_rows, block_count, block_side, block_side)
    result = jnp.einsum(
        "kbpq,bqo->kpo",
        rounded,
        orbitals.reshape(block_count, block_side, -1),
        preferred_element_type=jnp.float32,
    )
    return result.reshape(block_rows * block_side, -1)


def solution(mesh):
    placed = (
        P(("quartet", "pert"), None, None),
        P(("quartet", "pert"), None),
        P(("quartet", "pert"), None),
        P(),
    )
    return jax.shard_map(
        per_device,
        mesh=mesh,
        in_specs=placed,
        out_specs=P(("quartet", "pert"), None),
        check_vma=False,
    )
```

profile of v0, /device:TPU:1, one launch (start us, length us, event | category | flops | bytes accessed | tf_op | source)
XLA Modules:
  0.0 778.2 jit_solution(13114167859087825460)
XLA Ops:
  0.0 73.1 %all-gather = s32[256,4,4]{2,1,0:T(4,128)S(1)} all-gather(s32[1,4,4]{2,1,0:T(4,128)} %bitcast.258), channel_id=1, replica_groups=mesh['quartet'=128,'pert'=2] {'quartet','pert'}, dimensions={0}, use_global_device_ids=true | all-gather | bytes 16448 | tf_op jit(solution)/shard_map/all_gather | solution.py:113
  94.1 12.7 %gather_fusion.5 = s32[1536]{0:T(1024)S(1)} fusion(s32[256,24]{0,1:T(8,128)S(1)} %reshape.610, s32[1536]{0:T(1024)S(1)} %reshape.772), kind=kCustom, calls=%fused_computation.2.clone | custom fusion | bytes 24576 | tf_op jit(solution)/shard_map/jit(take_along_axis)/gather | solution.py:49
  106.8 12.7 %gather_fusion.6 = s32[1536]{0:T(1024)S(1)} fusion(s32[256,24]{0,1:T(8,128)S(1)} %reshape.611, s32[1536]{0:T(1024)S(1)} %reshape.772), kind=kCustom, calls=%fused_computation.3.clone | custom fusion | bytes 24576 | tf_op jit(solution)/shard_map/jit(take_along_axis)/gather | solution.py:50
  120.6 12.7 %gather_fusion.3 = s32[1536]{0:T(1024)S(1)} fusion(s32[256,24]{0,1:T(8,128)S(1)} %reshape.606, s32[1536]{0:T(1024)S(1)} %reshape.762), kind=kCustom, calls=%fused_computation.clone | custom fusion | bytes 24576 | tf_op jit(solution)/shard_map/jit(take_along_axis)/gather | solution.py:49
  133.3 12.7 %gather_fusion.4 = s32[1536]{0:T(1024)S(1)} fusion(s32[256,24]{0,1:T(8,128)S(1)} %reshape.607, s32[1536]{0:T(1024)S(1)} %reshape.762), kind=kCustom, calls=%fused_computation.1.clone | custom fusion | bytes 24576 | tf_op jit(solution)/shard_map/jit(take_along_axis)/gather | solution.py:50
  211.9 10.9 %reshape_squeeze.15 = bf16[32,32,32,32]{3,2,1,0:T(8,128)(2,1)} reshape(bf16[1,1024,1024]{2,1,0:T(8,128)(2,1)} %get-tuple-element.16) | data formatting | bytes 4194304 | tf_op jit(solution)/shard_map/reshape;squeeze | solution.py:66
  233.3 15.3 %copy.164 = bf16[32,32,32,32]{2,1,3,0:T(8,128)(2,1)} copy(bf16[32,32,32,32]{3,2,1,0:T(8,128)(2,1)} %reshape_squeeze.15) | data formatting | bytes 4194304 | tf_op jit(solution)/shard_map/reshape;squeeze | solution.py:66
  248.6 11.2 %reshape_squeeze.14 = bf16[32,32,32,32]{3,2,1,0:T(8,128)(2,1)} reshape(bf16[1,1024,1024]{2,1,0:T(8,128)(2,1)} %get-tuple-element.17) | data formatting | bytes 4194304 | tf_op jit(solution)/shard_map/reshape;squeeze | solution.py:66
  270.3 15.3 %copy.162 = bf16[32,32,32,32]{2,1,3,0:T(8,128)(2,1)} copy(bf16[32,32,32,32]{3,2,1,0:T(8,128)(2,1)} %reshape_squeeze.14) | data formatting | bytes 4194304 | tf_op jit(solution)/shard_map/reshape;squeeze | solution.py:66
  307.0 15.3 %copy.160 = bf16[32,32,32,32]{2,1,3,0:T(8,128)(2,1)} copy(bf16[32,32,32,32]{3,2,1,0:T(8,128)(2,1)} %reshape_squeeze.13) | data formatting | bytes 4194304 | tf_op jit(solution)/shard_map/reshape;squeeze | solution.py:66
  340.9 15.4 %copy.158 = bf16[32,32,32,32]{2,1,3,0:T(8,128)(2,1)} copy(bf16[32,32,32,32]{3,2,1,0:T(8,128)(2,1)} %reshape_squeeze.12) | data formatting | bytes 4194304 | tf_op jit(solution)/shard_map/reshape;squeeze | solution.py:66
  356.8 12.4 %reshape.621 = bf16[1024,1024]{1,0:T(8,128)(2,1)} reshape(bf16[32,32,32,32]{3,2,1,0:T(8,128)(2,1)} %bitcast.243) | data formatting | bytes 4194304 | tf_op jit(solution)/shard_map/reshape | solution.py:67
  369.2 12.4 %reshape.622 = bf16[1024,1024]{1,0:T(8,128)(2,1)} reshape(bf16[32,32,32,32]{3,2,1,0:T(8,128)(2,1)} %bitcast.242) | data formatting | bytes 4194304 | tf_op jit(solution)/shard_map/reshape | solution.py:68
  381.6 12.4 %reshape.619 = bf16[1024,1024]{1,0:T(8,128)(2,1)} reshape(bf16[32,32,32,32]{3,2,1,0:T(8,128)(2,1)} %bitcast.245) | data formatting | bytes 4194304 | tf_op jit(solution)/shard_map/reshape | solution.py:67
  394.0 12.8 %reshape.620 = bf16[1024,1024]{1,0:T(8,128)(2,1)} reshape(bf16[32,32,32,32]{3,2,1,0:T(8,128)(2,1)} %bitcast.244) | data formatting | bytes 4194304 | tf_op jit(solution)/shard_map/reshape | solution.py:68
  406.8 12.4 %reshape.617 = bf16[1024,1024]{1,0:T(8,128)(2,1)} reshape(bf16[32,32,32,32]{3,2,1,0:T(8,128)(2,1)} %bitcast.247) | data formatting | bytes 4194304 | tf_op jit(solution)/shard_map/reshape | solution.py:67
  419.2 12.4 %reshape.618 = bf16[1024,1024]{1,0:T(8,128)(2,1)} reshape(bf16[32,32,32,32]{3,2,1,0:T(8,128)(2,1)} %bitcast.246) | data formatting | bytes 4194304 | tf_op jit(solution)/shard_map/reshape | solution.py:68
  431.6 11.3 %reshape.615 = bf16[1024,1024]{1,0:T(8,128)(2,1)S(1)} reshape(bf16[32,32,32,32]{3,2,1,0:T(8,128)(2,1)} %bitcast.249) | data formatting | bytes 4194304 | tf_op jit(solution)/shard_map/reshape | solution.py:67
  443.0 12.4 %reshape.616 = bf16[1024,1024]{1,0:T(8,128)(2,1)} reshape(bf16[32,32,32,32]{3,2,1,0:T(8,128)(2,1)} %bitcast.248) | data formatting | bytes 4194304 | tf_op jit(solution)/shard_map/reshape | solution.py:68
  537.5 12.3 %copy.165 = f32[128,2,6,1024]{3,1,2,0:T(2,128)} copy(f32[128,2,6,1024]{3,2,1,0:T(8,128)} %reshape.624) | data formatting | bytes 12582912 | tf_op jit(solution)/shard_map/reshape | solution.py:171
  549.7 14.6 %all-to-all-start.2 = ((f32[128,2,6,1024]{3,1,2,0:T(2,128)}), f32[128,2,6,1024]{3,1,2,0:T(2,128)}, u32[]{:S(2)}, u32[]{:S(2)}) async-start(f32[128,2,6,1024]{3,1,2,0:T(2,128)} %copy.165), calls=%async_computation.2 | async-start | bytes 12582912 | tf_op jit(solution)/shard_map/all_to_all | solution.py:173
  564.6 137.0 %all-to-all-done.2 = f32[128,2,6,1024]{3,1,2,0:T(2,128)} async-done(((f32[128,2,6,1024]{3,1,2,0:T(2,128)}), f32[128,2,6,1024]{3,1,2,0:T(2,128)}, u32[]{:S(2)}, u32[]{:S(2)}) %all-to-all-start.2) | async-done | bytes 6291488 | tf_op jit(solution)/shard_map/all_to_all | solution.py:173
  708.1 13.7 %all_to_all.21 = f32[128,2,6,1024]{3,0,2,1:T(8,128)S(1)} all-to-all(f32[128,2,6,1024]{3,0,2,1:T(8,128)S(1)} %copy.166), channel_id=1, replica_groups=mesh['quartet'=128,'pert'=2] {'pert'}, dimensions={1} | all-to-all | bytes 12582912 | tf_op jit(solution)/shard_map/all_to_all | solution.py:172
  737.0 16.9 %scatter_custom_fusion = f32[1024,1024]{1,0:T(8,128)} fusion(s32[1536]{0:T(1024)S(1)} %reshape.681, f32[1536,1024]{1,0:T(8,128)} %reshape.683, f32[]{:T(128)} %constant.143.clone.1), kind=kCustom, calls=%fused_computation.29 | custom fusion | flops 1572864 | bytes 4194816 | tf_op jit(solution)/shard_map/scatter-add | solution.py:190
  (158 shorter events, 276.9 us)
Async XLA Ops:
  0.0 776.4 %copy-start = (bf16[2048,256]{1,0:T(8,128)(2,1)S(1)}, bf16[2048,256]{1,0:T(8,128)(2,1)}, u32[]{:S(2)}) copy-start(bf16[2048,256]{1,0:T(8,128)(2,1)} %param.9) | copy-start | bytes 3145732
  83.4 4.2 copy-start.11
  90.9 16.0 %copy-start.1 = (s32[256,24]{0,1:T(8,128)}, s32[256,24]{0,1:T(8,128)S(1)}, u32[]{:S(2)}) copy-start(s32[256,24]{0,1:T(8,128)S(1)} %reshape.610) | copy-start | bytes 73732
  92.6 0.6 copy-start.13
  92.6 27.6 %copy-start.15 = (s32[256,24]{0,1:T(8,128)}, s32[256,24]{0,1:T(8,128)S(1)}, u32[]{:S(2)}) copy-start(s32[256,24]{0,1:T(8,128)S(1)} %get-tuple-element.9) | copy-start | bytes 73732
  93.2 0.6 copy-start.17
  133.3 13.2 %copy-start.12 = (bf16[512,2048]{1,0:T(8,128)(2,1)S(1)}, bf16[512,2048]{1,0:T(8,128)(2,1)}, u32[]{:S(2)}) copy-start(bf16[512,2048]{1,0:T(8,128)(2,1)} %param.8) | copy-start | bytes 6291460
  170.0 2.9 copy-start.18
  196.3 264.5 %all-to-all-start = ((bf16[128,2,6,1024]{3,1,2,0:T(2,128)(2,1)}), bf16[128,2,6,1024]{3,1,2,0:T(2,128)(2,1)}, u32[]{:S(2)}, u32[]{:S(2)}) async-start(bf16[128,2,6,1024]{3,1,2,0:T(2,128)(2,1)} %copy.154), calls=%async_computation | async-start | bytes 6291456 | tf_op jit(solution)/shard_map/all_to_all | solution.py:139
  340.9 15.4 %copy-start.14 = (s32[256,24]{0,1:T(8,128)S(1)}, s32[256,24]{0,1:T(8,128)}, u32[]{:S(2)}) copy-start(s32[256,24]{0,1:T(8,128)} %copy-done.13) | copy-start | bytes 73732
  340.9 15.4 %copy-start.16 = (s32[256,24]{0,1:T(8,128)S(1)}, s32[256,24]{0,1:T(8,128)}, u32[]{:S(2)}) copy-start(s32[256,24]{0,1:T(8,128)} %copy-done.15) | copy-start | bytes 73732
  340.9 15.5 %copy-start.2 = (s32[256,24]{0,1:T(8,128)S(1)}, s32[256,24]{0,1:T(8,128)}, u32[]{:S(2)}) copy-start(s32[256,24]{0,1:T(8,128)} %copy-done.1) | copy-start | bytes 73732
  490.3 5.3 copy-start.10
  490.3 15.0 %slice-start = ((s8[8388608]{0:T(1024)(128)(4,1)}), s8[4194304]{0:T(1024)(128)(4,1)S(1)}, s32[]{:S(2)}) async-start(s8[8388608]{0:T(1024)(128)(4,1)} %bitcast.252), calls=%async_computation.4 | async-start | bytes 8388608
  497.9 4.8 copy-start.8
  500.5 3.0 copy-start.9
  500.5 4.8 slice-start.1
  504.7 1.6 copy-start.6
  505.3 1.8 copy-start.7
  508.4 1.6 copy-start.4
  508.9 1.9 copy-start.5
  512.5 1.6 copy-start.3
  549.7 14.6 %copy-start.19 = (s32[256,6]{0,1:T(8,128)S(1)}, s32[256,6]{0,1:T(8,128)}, u32[]{:S(2)}) copy-start(s32[256,6]{0,1:T(8,128)} %get-tuple-element.25) | copy-start | bytes 18436
  549.7 151.9 %all-to-all-start.2 = ((f32[128,2,6,1024]{3,1,2,0:T(2,128)}), f32[128,2,6,1024]{3,1,2,0:T(2,128)}, u32[]{:S(2)}, u32[]{:S(2)}) async-start(f32[128,2,6,1024]{3,1,2,0:T(2,128)} %copy.165), calls=%async_computation.2 | async-start | bytes 12582912 | tf_op jit(solution)/shard_map/all_to_all | solution.py:173
where the time goes:
time: 793 us; the launch traced here: 778 us
  local copies, waits for them, and re-layouts  468 us (59%)
  waiting for transfers between devices  137 us (17%)
  blocking collectives  93.1 us (12%)
  other arithmetic  29.8 us (4%)
  matrix products  25.3 us (3%)
  starting transfers between devices  24.4 us (3%)
    another operation x12, local copies, waits for them, and re-layouts, digest(): integral.reshape(block_side, block_side, block_side, block_side)  144 us
    all_to_all x1, waiting for transfers between devices, per_device(): lax.all_to_all(leaving, 'quartet', split_axis=0, concat_axis=0, tiled=True)  137 us
    all_gather x1, blocking collectives, per_device(): lax.all_gather(quartets, ('quartet', 'pert'), axis=0, tiled=True)  73.1 us
    reshape x4, local copies, waits for them, and re-layouts, digest(): paired_pt = integral_four.transpose(0, 3, 1, 2).reshape(area, area)  50 us
    reshape x4, local copies, waits for them, and re-layouts, digest(): paired_ps = integral_four.transpose(0, 2, 1, 3).reshape(area, area)  48.5 us
    gather x10, local copies, waits for them, and re-layouts, owner_lookup(): jnp.take_along_axis(rows, chosen, axis=1)  26.4 us
    gather x6, local copies, waits for them, and re-layouts, owner_lookup(): jnp.take_along_axis(cols, chosen, axis=1)  25.9 us
    reshape x2, local copies, waits for them, and re-layouts, per_device(): fock_terms[inverse].reshape(quartet_size, pert_size, capacity, tile_area)  20.3 us
  transfers between devices with their start and end apart: 2, of which 1 were waited for; matrix products, arithmetic and copies ran while one was open for 33% of the time, Pallas kernels for 0%

commit v1 on v0

v1 whole, which is shorter than its diff:
```python
import functools

import jax
import jax.numpy as jnp
from jax import lax
from jax.experimental import pallas as pl
from jax.experimental.pallas import tpu as pltpu
from jax.sharding import PartitionSpec as P

P_SIZE = 64
S = 32
NB = 64
QUARTERS = 4
SPAN = NB // QUARTERS
GROUP = 4
SLOTS = 6
LANES = 128
SUB = 8
AREA = S * S
CHUNK = SLOTS * SUB
SCALE = 32.0

f32 = jnp.float32
bf16 = jnp.bfloat16
f16 = jnp.float16


def swap_groups(parts):
    lane = lax.broadcasted_iota(jnp.int32, parts[0].shape, len(parts[0].shape) - 1)
    axis = len(parts[0].shape) - 1
    low_half = lane < 64
    even = (lane // 32) % 2 == 0
    v0, v1, v2, v3 = parts
    u0 = jnp.where(low_half, v0, pltpu.roll(v2, 64, axis))
    u2 = jnp.where(low_half, pltpu.roll(v0, 64, axis), v2)
    u1 = jnp.where(low_half, v1, pltpu.roll(v3, 64, axis))
    u3 = jnp.where(low_half, pltpu.roll(v1, 64, axis), v3)
    w0 = jnp.where(even, u0, pltpu.roll(u1, 32, axis))
    w1 = jnp.where(even, pltpu.roll(u0, 96, axis), u1)
    w2 = jnp.where(even, u2, pltpu.roll(u3, 32, axis))
    w3 = jnp.where(even, pltpu.roll(u2, 96, axis), u3)
    return [w0, w1, w2, w3]


def tiles_kernel(dens_ref, tiles_ref, turned_ref, rows_ref, flip_ref):
    rows_ref[...] = dens_ref[...].astype(f32)
    for a in range(SPAN):
        parts = [rows_ref[pl.ds(S * a + s, SUB, stride=4), :] for s in range(4)]
        for b, tile in enumerate(swap_groups(parts)):
            tiles_ref[b * SPAN + a] = tile
    for big in range(4):
        flip_ref[...] = rows_ref[LANES * big : LANES * (big + 1), :].T
        for b in range(4):
            parts = [flip_ref[pl.ds(S * b + t, SUB, stride=4), :] for t in range(4)]
            for a, tile in enumerate(swap_groups(parts)):
                turned_ref[b * SPAN + 4 * big + a] = tile


def cut_tiles(density):
    rows, columns = density.shape
    steps = columns // LANES
    tiles = jax.ShapeDtypeStruct((NB * SPAN, SUB, LANES), f32)
    block = pl.BlockSpec((4 * SPAN, SUB, LANES), lambda i: (i, 0, 0))
    return pl.pallas_call(
        tiles_kernel,
        grid=(steps,),
        in_specs=[pl.BlockSpec((rows, LANES), lambda i: (0, i))],
        out_specs=[block, block],
        out_shape=[tiles, tiles],
        scratch_shapes=[pltpu.VMEM((rows, LANES), f32), pltpu.VMEM((LANES, LANES), f32)],
        name="cut_tiles",
    )(density)


def pick_kernel(index_ref, tiles_ref, turned_ref, out_ref):
    per_step = out_ref.shape[0]
    first = pl.program_id(0) * per_step

    def one(n, carry):
        e = first + n
        at = [index_ref[r, e] for r in range(SLOTS)]
        pairs = (
            (tiles_ref[at[0]], turned_ref[at[1]]),
            (tiles_ref[at[2]], turned_ref[at[3]]),
            (tiles_ref[at[4]], tiles_ref[at[5]]),
        )
        for r, pair in enumerate(pairs):
            out_ref[n, 16 * r : 16 * (r + 1), :] = jnp.concatenate(pair, axis=0).astype(bf16)
        return carry

    lax.fori_loop(0, per_step, one, 0, unroll=4)


def pick_tiles(index, tiles, turned):
    devices = index.shape[1]
    per_step = 32
    whole = pl.BlockSpec(tiles.shape, lambda i, index: (0, 0, 0))
    return pl.pallas_call(
        pick_kernel,
        grid_spec=pltpu.PrefetchScalarGridSpec(
            num_scalar_prefetch=1,
            grid=(devices // per_step,),
            in_specs=[whole, whole],
            out_specs=pl.BlockSpec((per_step, CHUNK, LANES), lambda i, index: (i, 0, 0)),
        ),
        out_shape=jax.ShapeDtypeStruct((devices, CHUNK, LANES), bf16),
        compiler_params=pltpu.CompilerParams(vmem_limit_bytes=40 << 20),
        name="pick_tiles",
    )(index, tiles, turned)


def pairings_kernel(g_ref, ps_ref, sp_ref, rows_ref):
    rows_ref[...] = g_ref[0].astype(f32)
    for big in range(8):
        lanes = slice(LANES * big, LANES * (big + 1))
        parts = [g_ref[0, S * (4 * big + p) : S * (4 * big + p + 1), :] for p in range(4)]
        for s, block in enumerate(swap_groups(parts)):
            sp_ref[0, S * s : S * (s + 1), lanes] = block
        parts = [rows_ref[pl.ds(4 * big + r, S, stride=S), :].astype(bf16) for r in range(4)]
        for s, block in enumerate(swap_groups(parts)):
            ps_ref[0, S * s : S * (s + 1), lanes] = block


def pairings(integrals):
    count = integrals.shape[0]
    shape = jax.ShapeDtypeStruct(integrals.shape, bf16)
    block = pl.BlockSpec((1, LANES, AREA), lambda m, c: (m, c, 0))
    return pl.pallas_call(
        pairings_kernel,
        grid=(count, AREA // LANES),
        in_specs=[pl.BlockSpec((1, AREA, LANES), lambda m, c: (m, 0, c))],
        out_specs=[block, block],
        out_shape=[shape, shape],
        scratch_shapes=[pltpu.VMEM((AREA, LANES), f32)],
        cost_estimate=pl.CostEstimate(
            flops=40_000_000_000, bytes_accessed=3 * 2 * count * AREA * AREA, transcendentals=0
        ),
        name="pairings",
    )(integrals)


def digest_kernel(quarter_ref, recv_ref, g_ref, ps_ref, sp_ref, out_ref, rows_ref):
    m = pl.program_id(0)

    @pl.when(m == 0)
    def _():
        def widen(x, carry):
            at = pl.multiple_of(x * QUARTERS * CHUNK, QUARTERS * CHUNK)
            rows_ref[pl.ds(at, QUARTERS * CHUNK), :] = recv_ref[
                pl.ds(at, QUARTERS * CHUNK), :
            ].astype(f32)
            return carry

        lax.fori_loop(0, P_SIZE, widen, 0)

    stride = QUARTERS * CHUNK
    q_i, q_j, q_k = (quarter_ref[3 * m + role] for role in range(3))

    def fetch(quarter, slot):
        first = quarter * CHUNK + slot * SUB
        return jnp.concatenate(
            [
                rows_ref[pl.ds(first + c, P_SIZE, stride=stride), :].astype(bf16)
                for c in range(SUB)
            ],
            axis=1,
        )

    def put(quarter, slot, value):
        first = quarter * CHUNK + slot * SUB
        for c in range(SUB):
            out_ref[pl.ds(first + c, P_SIZE, stride=stride), :] = value[
                :, LANES * c : LANES * (c + 1)
            ]

    def times(left, right):
        return jnp.dot(left, right, preferred_element_type=f32)

    def times_turned(left, right):
        return lax.dot_general(
            left, right, (((1,), (1,)), ((), ())), preferred_element_type=f32
        )

    g, ps, sp = g_ref[0], ps_ref[0], sp_ref[0]
    half = -0.5 * SCALE
    put(q_i, 0, SCALE * times_turned(fetch(q_k, 4), g))
    put(q_k, 4, SCALE * times(fetch(q_i, 0), g))
    put(q_i, 1, half * times_turned(fetch(q_j, 2), ps))
    put(q_j, 2, half * times(fetch(q_i, 1), ps))
    put(q_i, 5, half * times(fetch(q_j, 3), sp))
    put(q_j, 3, half * times_turned(fetch(q_i, 5), sp))


def digest(quarters, received, integrals, ps, sp):
    count = integrals.shape[0]
    rows = received.shape[0]
    square = pl.BlockSpec((1, AREA, AREA), lambda m, q: (m, 0, 0))
    whole = pl.BlockSpec((rows, LANES), lambda m, q: (0, 0))
    return pl.pallas_call(
        digest_kernel,
        grid_spec=pltpu.PrefetchScalarGridSpec(
            num_scalar_prefetch=1,
            grid=(count,),
            in_specs=[whole, square, square, square],
            out_specs=whole,
            scratch_shapes=[pltpu.VMEM((rows, LANES), f32)],
        ),
        out_shape=jax.ShapeDtypeStruct((rows, LANES), f32),
        compiler_params=pltpu.CompilerParams(vmem_limit_bytes=56 << 20),
        name="digest",
    )(quarters, received, integrals, ps, sp)


def finish_kernel(
    index_ref, recv_ref, orb_ref, out_ref, tiles_ref, turned_ref, rows_ref, flip_ref, fock_ref
):
    step = pl.program_id(0)
    per_step = recv_ref.shape[0]

    @pl.when(step == 0)
    def _():
        tiles_ref[...] = jnp.zeros_like(tiles_ref)
        turned_ref[...] = jnp.zeros_like(turned_ref)

    def one(n, carry):
        e = step * per_step + n
        for slot, target in enumerate(
            (tiles_ref, turned_ref, tiles_ref, turned_ref, tiles_ref, tiles_ref)
        ):
            at = index_ref[slot, e]
            target[at] = target[at] + recv_ref[n, SUB * slot : SUB * (slot + 1), :]
        return carry

    lax.fori_loop(0, per_step, one, 0, unroll=4)

    @pl.when(step == pl.num_programs(0) - 1)
    def _():
        def column(c, carry):
            base = c * 4 * SPAN
            for a in range(SPAN):
                parts = [tiles_ref[base + b * SPAN + a] for b in range(4)]
                for s, block in enumerate(swap_groups(parts)):
                    rows_ref[pl.ds(S * a + s, SUB, stride=4), :] = block
            for big in range(4):
                for b in range(4):
                    parts = [turned_ref[base + b * SPAN + 4 * big + a] for a in range(4)]
                    for t, block in enumerate(swap_groups(parts)):
                        flip_ref[pl.ds(S * b + t, SUB, stride=4), :] = block
                rows = slice(LANES * big, LANES * (big + 1))
                total = rows_ref[rows, :] + flip_ref[...].T
                fock_ref[rows, pl.ds(pl.multiple_of(c * LANES, LANES), LANES)] = (
                    total * (1.0 / SCALE)
                ).astype(bf16)
            return carry

        lax.fori_loop(0, NB // 4, column, 0)
        out_ref[...] = jnp.dot(fock_ref[...], orb_ref[...], preferred_element_type=f32)


def finish(index, arrived, orbitals, rows):
    devices = index.shape[1]
    per_step = 32
    basis, occupied = orbitals.shape
    return pl.pallas_call(
        finish_kernel,
        grid_spec=pltpu.PrefetchScalarGridSpec(
            num_scalar_prefetch=1,
            grid=(devices // per_step,),
            in_specs=[
                pl.BlockSpec((per_step, CHUNK, LANES), lambda i, index: (i, 0, 0)),
                pl.BlockSpec((basis, occupied), lambda i, index: (0, 0)),
            ],
            out_specs=pl.BlockSpec((rows, occupied), lambda i, index: (0, 0)),
            scratch_shapes=[
                pltpu.VMEM((NB * SPAN, SUB, LANES), f32),
                pltpu.VMEM((NB * SPAN, SUB, LANES), f32),
                pltpu.VMEM((rows, LANES), f32),
                pltpu.VMEM((LANES, LANES), f32),
                pltpu.VMEM((rows, basis), bf16),
            ],
        ),
        out_shape=jax.ShapeDtypeStruct((rows, occupied), f32),
        compiler_params=pltpu.CompilerParams(vmem_limit_bytes=40 << 20),
        name="finish",
    )(index, arrived, orbitals)


def tile_index(lists, quarter):
    i, j, k, l = (lists[:, :, role] for role in range(4))
    low = quarter * SPAN
    of_i = i // SPAN == quarter
    of_j = j // SPAN == quarter
    of_k = k // SPAN == quarter

    def pick(mask, value):
        return jnp.sum(jnp.where(mask, value, 0), axis=0)

    return jnp.stack(
        [
            pick(of_i, j * SPAN + i - low),
            pick(of_i, k * SPAN + i - low),
            pick(of_j, l * SPAN + j - low),
            pick(of_j, k * SPAN + j - low),
            pick(of_k, l * SPAN + k - low),
            pick(of_i, l * SPAN + i - low),
        ]
    )


def per_device(integrals, quartets, density, orbitals):
    axes = ("quartet", "pert")
    devices = lax.axis_size("quartet") * lax.axis_size("pert")
    myself = lax.axis_index("quartet") * lax.axis_size("pert") + lax.axis_index("pert")
    quarter = myself % QUARTERS

    flat = jnp.pad(quartets.reshape(1, GROUP * 4), ((0, 0), (0, LANES - GROUP * 4)))
    gathered = lax.all_gather(jnp.broadcast_to(flat, (SUB, LANES)), axes, axis=0, tiled=True)
    tiles, turned = cut_tiles(density)
    lists = gathered.reshape(devices, SUB, LANES)[:, 0, : GROUP * 4].T.reshape(GROUP, 4, devices)
    index = tile_index(lists.transpose(0, 2, 1), quarter)

    outgoing = pick_tiles(index, tiles, turned)
    received = lax.all_to_all(outgoing, axes, 0, 0, tiled=True)
    ps, sp = pairings(integrals)
    quarters = (quartets[:, :3] // SPAN).reshape(-1)
    terms = digest(quarters, received.reshape(-1, LANES), integrals, ps, sp)
    leaving = terms.astype(f16).reshape(devices, CHUNK, LANES)
    landed = lax.all_to_all(leaving, axes, 0, 0, tiled=True)
    return finish(index, landed.astype(f32), orbitals, density.shape[0])


def solution(mesh):
    placed = (
        P(("quartet", "pert"), None, None),
        P(("quartet", "pert"), None),
        P(("quartet", "pert"), None),
        P(),
    )
    return jax.shard_map(
        per_device,
        mesh=mesh,
        in_specs=placed,
        out_specs=P(("quartet", "pert"), None),
        check_vma=False,
    )
```

time: 793 us -> 367 us (0.46); the launches traced: 778 us -> 365 us
  local copies, waits for them, and re-layouts: 468 us -> 10.2 us
  Pallas kernels: 0 us -> 122 us
  other arithmetic: 29.8 us -> 3.63 us
  matrix products: 25.3 us -> 0 us
  starting transfers between devices: 24.4 us -> 10.4 us
  waiting for transfers between devices: 137 us -> 124 us
  between operations: 0.89 us -> 13.5 us
  blocking collectives: 93.1 us -> 81.8 us
    reshape x23 -> x3, local copies, waits for them, and re-layouts: 174 us -> 1.37 us  [the longest x1 0.76 us: per_device(): quartets.reshape(1, GROUP * 4)]
    another operation x20 -> x1, local copies, waits for them, and re-layouts: 161 us -> 0.03 us  [tile_index(): jnp.stack([pick(of_i, j * SPAN + i - low), pick(of_i, k * SPAN + i - low)...]
    pallas_call x0 -> x5, Pallas kernels: none -> 122 us  [the longest x1 36.3 us: pairings(): pl.pallas_call(pairings_kernel, grid=(count, AREA // LANES), in_specs=[pl...]
    all_to_all x2 -> x1, waiting for transfers between devices: 137 us -> 38.7 us  [per_device(): received = lax.all_to_all(outgoing, axes, 0, 0, tiled=True)]
    all_gather x0 -> x1, waiting for transfers between devices: none -> 85.5 us  [per_device(): lax.all_gather(jnp.broadcast_to(flat, (SUB, LANES)), axes, axis=0, tiled=...]
    gather x19 -> x0, local copies, waits for them, and re-layouts: 79 us -> none  [the longest x10 26.4 us: owner_lookup(): jnp.take_along_axis(rows, chosen, axis=1)]
    all_gather x1 -> x0, blocking collectives: 73.1 us -> none  [per_device(): lax.all_gather(quartets, ('quartet', 'pert'), axis=0, tiled=True)]
    all_to_all x2 -> x1, blocking collectives: 20 us -> 81.8 us  [per_device(): landed = lax.all_to_all(leaving, axes, 0, 0, tiled=True)]
  transfers between devices with their start and end apart: 2 -> 2, of which waited for: 1 -> 2; matrix products, arithmetic and copies ran while one was open for 33% -> 0% of each run, Pallas kernels for 0% -> 16%
where the time goes in v1:
time: 367 us; the launch traced here: 365 us
  waiting for transfers between devices  124 us (34%)
  Pallas kernels  122 us (33%)
  blocking collectives  81.8 us (22%)
  between operations  13.5 us (4%)
  starting transfers between devices  10.4 us (3%)
  local copies, waits for them, and re-layouts  10.2 us (3%)
    all_gather x1, waiting for transfers between devices, per_device(): lax.all_gather(jnp.broadcast_to(flat, (SUB, LANES)), axes, axis=0, tiled=...  85.5 us
    all_to_all x1, blocking collectives, per_device(): landed = lax.all_to_all(leaving, axes, 0, 0, tiled=True)  81.8 us
    all_to_all x1, waiting for transfers between devices, per_device(): received = lax.all_to_all(outgoing, axes, 0, 0, tiled=True)  38.7 us
    pallas_call x1, Pallas kernels, pairings(): pl.pallas_call(pairings_kernel, grid=(count, AREA // LANES), in_specs=[pl...  36.3 us
    pallas_call x1, Pallas kernels, finish(): pl.pallas_call(finish_kernel, grid_spec=pltpu.PrefetchScalarGridSpec(num_...  31.1 us
    pallas_call x1, Pallas kernels, digest(): pl.pallas_call(digest_kernel, grid_spec=pltpu.PrefetchScalarGridSpec(num_...  25 us
    pallas_call x1, Pallas kernels, cut_tiles(): pl.pallas_call(tiles_kernel, grid=(steps,), in_specs=[pl.BlockSpec((rows,...  24 us
    all_to_all x1, starting transfers between devices, per_device(): received = lax.all_to_all(outgoing, axes, 0, 0, tiled=True)  10.4 us
  transfers between devices with their start and end apart: 2, of which 2 were waited for; matrix products, arithmetic and copies ran while one was open for 0% of the time, Pallas kernels for 16%

profile of v1, /device:TPU:1, one launch (start us, length us, event | category | flops | bytes accessed | tf_op | source)
XLA Modules:
  0.0 365.5 jit_solution(6740864008681791735)
XLA Ops:
  6.5 0.0 all-gather.2.cloned.1.call-start
  6.5 0.8 reshape.20
  7.3 0.6 broadcast_in_dim.15
  7.9 0.0 all-gather.2.cloned.1.call-update
  7.9 24.0 %cut_tiles.1 = (f32[1024,8,128]{2,1,0:T(8,128)}, f32[1024,8,128]{2,1,0:T(8,128)}) custom-call(bf16[512,2048]{1,0:T(8,128)(2,1)} %dens_ref.1), custom_call_target="tpu_custom_call" | custom-call | tf_op jit(solution)/shard_map/cut_tiles/pallas_call | solution.py:64
  32.0 85.5 %all-gather.2.cloned.1.call-done = s32[2048,128]{1,0:T(8,128)} async-done(((s32[8,128]{1,0:T(8,128)}), s32[2048,128]{1,0:T(8,128)}) %all-gather.2.cloned.1.call-update) | async-done | bytes 1048592 | tf_op jit(solution)/shard_map/all_gather | solution.py:317
  117.4 1.3 slice.24
  118.7 0.1 copy.10
  118.8 0.1 fusion.14
  118.9 2.2 copy-done
  121.1 2.2 copy-done.1
  123.3 5.4 %pick_tiles.1 = bf16[256,48,128]{2,1,0:T(8,128)(2,1)} custom-call(s32[6,256]{1,0:T(8,128)S(1)} %stack.27.index_ref, f32[1024,8,128]{2,1,0:T(8,128)S(1)} %copy-done, f32[1024,8,128]{2,1,0:T(8,128)S(1)} %copy-done.1), custom_call_target="tpu_custom_call" | custom-call | tf_op jit(solution)/shard_map/pick_tiles/pallas_call | solution.py:98
  128.7 10.4 %all-to-all-start = ((bf16[256,48,128]{2,1,0:T(8,128)(2,1)}), bf16[256,48,128]{2,1,0:T(8,128)(2,1)S(1)}, u32[]{:S(2)}, u32[]{:S(2)}) async-start(bf16[256,48,128]{2,1,0:T(8,128)(2,1)} %pick_tiles.1), calls=%async_computation | async-start | bytes 6291456 | tf_op jit(solution)/shard_map/all_to_all | solution.py:323
  139.2 0.0 copy-done.4
  139.2 0.6 reshape.23.quarter_ref
  139.8 36.3 %pairings.1 = (bf16[4,1024,1024]{2,1,0:T(8,128)(2,1)}, bf16[4,1024,1024]{2,1,0:T(8,128)(2,1)}) custom-call(bf16[4,1024,1024]{2,1,0:T(8,128)(2,1)} %g_ref.3), custom_call_target="tpu_custom_call" | custom-call | flops 40000000000 | bytes 25165824 | tf_op jit(solution)/shard_map/pairings/pallas_call | solution.py:128
  176.0 38.7 %all-to-all-done = bf16[256,48,128]{2,1,0:T(8,128)(2,1)S(1)} async-done(((bf16[256,48,128]{2,1,0:T(8,128)(2,1)}), bf16[256,48,128]{2,1,0:T(8,128)(2,1)S(1)}, u32[]{:S(2)}, u32[]{:S(2)}) %all-to-all-start) | async-done | bytes 3145760 | tf_op jit(solution)/shard_map/all_to_all | solution.py:323
  214.8 1.7 copy-done.3
  216.5 25.0 %digest.1 = f32[12288,128]{1,0:T(8,128)} custom-call(s32[12]{0:T(128)} %reshape.23.quarter_ref, bf16[12288,128]{1,0:T(8,128)(2,1)} %bitcast.85, bf16[4,1024,1024]{2,1,0:T(8,128)(2,1)} %g_ref.3, bf16[4,1024,1024]{2,1,0:T(8,128)(2,1)} %get-tuple-element.11.ps_ref, bf16[4,1024,1024]{2,1,0:T(8,128)(2,1)} %get-tuple-element.12.sp_ref), custom_call_target="tpu_custom_call" | custom-call | tf_op jit(solution)/shard_map/digest/pallas_call | solution.py:199
  241.4 3.1 convert_element_type.6
  244.5 81.8 %all_to_all.10 = f16[256,48,128]{2,1,0:T(8,128)(2,1)S(1)} all-to-all(f16[256,48,128]{2,1,0:T(8,128)(2,1)S(1)} %bitcast.86), channel_id=1, replica_groups=mesh['quartet'=128,'pert'=2] {'quartet','pert'}, dimensions={0} | all-to-all | bytes 6291456 | tf_op jit(solution)/shard_map/all_to_all | solution.py:328
  326.3 0.5 convert_element_type.7.recv_ref
  326.8 0.7 copy-done.2
  327.5 31.1 %finish.1 = f32[512,256]{1,0:T(8,128)} custom-call(s32[6,256]{1,0:T(8,128)S(1)} %stack.27.index_ref, f32[256,48,128]{2,1,0:T(8,128)S(1)} %convert_element_type.7.recv_ref, bf16[2048,256]{1,0:T(8,128)(2,1)S(1)} %copy-done.2), custom_call_target="tpu_custom_call" | custom-call | tf_op jit(solution)/shard_map/finish/pallas_call | solution.py:264
  (10 shorter events, 0.1 us)
Async XLA Ops:
  6.5 110.9 %all-gather.2.cloned.1.call-start = ((), (), s32[]{:S(2)}) async-start(), calls=%async_computation.2 | async-start | bytes 1052672 | tf_op jit(solution)/shard_map/all_gather | solution.py:317
  118.9 2.2 copy-start
  121.1 2.2 copy-start.1
  128.7 10.4 %copy-start.4 = (s32[4,4]{1,0:T(4,128)S(1)}, s32[4,4]{1,0:T(4,128)}, u32[]{:S(2)}) copy-start(s32[4,4]{1,0:T(4,128)} %param.5) | copy-start | bytes 196
  128.7 86.0 %all-to-all-start = ((bf16[256,48,128]{2,1,0:T(8,128)(2,1)}), bf16[256,48,128]{2,1,0:T(8,128)(2,1)S(1)}, u32[]{:S(2)}, u32[]{:S(2)}) async-start(bf16[256,48,128]{2,1,0:T(8,128)(2,1)} %pick_tiles.1), calls=%async_computation | async-start | bytes 6291456 | tf_op jit(solution)/shard_map/all_to_all | solution.py:323
  214.8 1.7 copy-start.3
  326.3 1.2 copy-start.2
Sparse Core Ops, SparseCore 0:
  11.1 106.3 all-gather.1

commit v2 on v1

v2 whole, which is shorter than its diff:
```python
import jax
import jax.numpy as jnp
import numpy as np
from jax import lax
from jax.experimental import pallas as pl
from jax.experimental.pallas import tpu as pltpu
from jax.sharding import PartitionSpec as P

P_SIZE = 64
S = 32
NB = 64
QUARTERS = 4
SPAN = NB // QUARTERS
GROUP = 4
SLOTS = 6
LANES = 128
SUB = 8
AREA = S * S
CHUNK = SLOTS * SUB
SCALE = 32.0

f32 = jnp.float32
bf16 = jnp.bfloat16
f16 = jnp.float16


def group_swap():
    eye = np.eye(4 * LANES, dtype=np.float32)
    return jnp.asarray(eye.reshape(4, 4, S, 4 * LANES).transpose(1, 0, 2, 3).reshape(eye.shape), bf16)


def times(left, right):
    return jnp.dot(left, right, preferred_element_type=f32)


def times_turned(left, right):
    return lax.dot_general(left, right, (((1,), (1,)), ((), ())), preferred_element_type=f32)


def tiles_kernel(dens_ref, swap_ref, tiles_ref, rows_ref):
    width = dens_ref.shape[1] // LANES
    parts = []
    for n in range(width):
        rows_ref[n] = dens_ref[:, LANES * n : LANES * (n + 1)].astype(f32)
        parts.append(
            jnp.concatenate(
                [rows_ref[n, pl.ds(s, LANES, stride=4), :].astype(bf16) for s in range(4)], axis=1
            )
        )
    out = times(jnp.concatenate(parts, axis=0), swap_ref[...])
    for n in range(width):
        for b in range(4):
            tiles_ref[(4 * n + b) * SPAN : (4 * n + b + 1) * SPAN] = out[
                LANES * n : LANES * (n + 1), LANES * b : LANES * (b + 1)
            ].reshape(SPAN, SUB, LANES)


def cut_tiles(density, swap):
    rows, columns = density.shape
    width = 2
    return pl.pallas_call(
        tiles_kernel,
        grid=(columns // (width * LANES),),
        in_specs=[
            pl.BlockSpec((rows, width * LANES), lambda i: (0, i)),
            pl.BlockSpec(swap.shape, lambda i: (0, 0)),
        ],
        out_specs=pl.BlockSpec((width * 4 * SPAN, SUB, LANES), lambda i: (i, 0, 0)),
        out_shape=jax.ShapeDtypeStruct((NB * SPAN, SUB, LANES), f32),
        scratch_shapes=[pltpu.VMEM((width, rows, LANES), f32)],
        cost_estimate=pl.CostEstimate(
            flops=4_000_000_000, bytes_accessed=6 * rows * columns, transcendentals=0
        ),
        name="cut_tiles",
    )(density, swap)


def pick_kernel(index_ref, tiles_ref, out_ref):
    per_step = out_ref.shape[0]
    first = pl.program_id(0) * per_step

    def one(n, carry):
        for pair in range(SLOTS // 2):
            halves = [tiles_ref[index_ref[2 * pair + h, first + n]] for h in range(2)]
            out_ref[n, 16 * pair : 16 * (pair + 1), :] = jnp.concatenate(halves, axis=0).astype(
                bf16
            )
        return carry

    lax.fori_loop(0, per_step, one, 0, unroll=8)


def pick_tiles(index, tiles):
    devices = index.shape[1]
    per_step = 64
    return pl.pallas_call(
        pick_kernel,
        grid_spec=pltpu.PrefetchScalarGridSpec(
            num_scalar_prefetch=1,
            grid=(devices // per_step,),
            in_specs=[pl.BlockSpec(memory_space=pltpu.VMEM)],
            out_specs=pl.BlockSpec((per_step, CHUNK, LANES), lambda i, index: (i, 0, 0)),
        ),
        out_shape=jax.ShapeDtypeStruct((devices, CHUNK, LANES), bf16),
        compiler_params=pltpu.CompilerParams(vmem_limit_bytes=58 << 20),
        name="pick_tiles",
    )(index, tiles)


def pairings_kernel(g_ref, swap_ref, ps_ref, rs_ref, rows_ref, ps_rows, rs_rows):
    step = pl.program_id(1)
    rows_ref[...] = g_ref[0].astype(f32)
    swap = swap_ref[...]

    def spread(parts, target):
        out = times(jnp.concatenate(parts, axis=1), swap)
        for big in range(8):
            for s in range(4):
                target[big, pl.ds(4 * step + s, S, stride=S), :] = out[
                    S * big : S * (big + 1), LANES * s : LANES * (s + 1)
                ]

    spread(
        [
            jnp.concatenate(
                [rows_ref[pl.ds(4 * big + r, S, stride=S), :] for big in range(8)], axis=0
            ).astype(bf16)
            for r in range(4)
        ],
        ps_rows,
    )
    spread(
        [
            jnp.concatenate(
                [g_ref[0, S * (4 * big + p) : S * (4 * big + p + 1), :] for big in range(8)],
                axis=0,
            )
            for p in range(4)
        ],
        rs_rows,
    )

    @pl.when(step == pl.num_programs(1) - 1)
    def _():
        for big in range(8):
            lanes = slice(LANES * big, LANES * (big + 1))
            ps_ref[0, :, lanes] = ps_rows[big].astype(bf16)
            rs_ref[0, :, lanes] = rs_rows[big].astype(bf16)


def pairings(integrals, swap):
    count = integrals.shape[0]
    shape = jax.ShapeDtypeStruct(integrals.shape, bf16)
    block = pl.BlockSpec((1, AREA, AREA), lambda m, c: (m, 0, 0))
    return pl.pallas_call(
        pairings_kernel,
        grid=(count, AREA // LANES),
        in_specs=[
            pl.BlockSpec((1, AREA, LANES), lambda m, c: (m, 0, c)),
            pl.BlockSpec(swap.shape, lambda m, c: (0, 0)),
        ],
        out_specs=[block, block],
        out_shape=[shape, shape],
        scratch_shapes=[pltpu.VMEM((AREA, LANES), f32)]
        + [pltpu.VMEM((AREA // LANES, AREA, LANES), f32)] * 2,
        compiler_params=pltpu.CompilerParams(vmem_limit_bytes=56 << 20),
        cost_estimate=pl.CostEstimate(
            flops=40_000_000_000, bytes_accessed=3 * 2 * count * AREA * AREA, transcendentals=0
        ),
        name="pairings",
    )(integrals, swap)


def digest_kernel(quarter_ref, recv_ref, g_ref, ps_ref, rs_ref, out_ref, rows_ref):
    m = pl.program_id(0)

    @pl.when(m == 0)
    def _():
        def widen(x, carry):
            at = pl.multiple_of(x * QUARTERS * CHUNK, QUARTERS * CHUNK)
            rows_ref[pl.ds(at, QUARTERS * CHUNK), :] = recv_ref[
                pl.ds(at, QUARTERS * CHUNK), :
            ].astype(f32)
            return carry

        lax.fori_loop(0, P_SIZE, widen, 0)

    stride = QUARTERS * CHUNK
    q_i, q_j, q_k = (quarter_ref[3 * m + role] for role in range(3))

    def fetch(quarter, slot):
        first = quarter * CHUNK + slot * SUB
        return jnp.concatenate(
            [
                rows_ref[pl.ds(first + c, P_SIZE, stride=stride), :].astype(bf16)
                for c in range(SUB)
            ],
            axis=1,
        )

    def put(quarter, slot, value):
        first = quarter * CHUNK + slot * SUB
        for c in range(SUB):
            out_ref[pl.ds(first + c, P_SIZE, stride=stride), :] = value[
                :, LANES * c : LANES * (c + 1)
            ]

    g, ps, rs = g_ref[0], ps_ref[0], rs_ref[0]
    half = -0.5 * SCALE
    put(q_i, 0, SCALE * times_turned(fetch(q_k, 4), g))
    put(q_k, 4, SCALE * times(fetch(q_i, 0), g))
    put(q_i, 1, half * times_turned(fetch(q_j, 2), ps))
    put(q_j, 2, half * times(fetch(q_i, 1), ps))
    put(q_i, 5, half * times(fetch(q_j, 3), rs))
    put(q_j, 3, half * times_turned(fetch(q_i, 5), rs))


def digest(quarters, received, integrals, ps, rs):
    count = integrals.shape[0]
    rows = received.shape[0]
    square = pl.BlockSpec((1, AREA, AREA), lambda m, q: (m, 0, 0))
    whole = pl.BlockSpec(memory_space=pltpu.VMEM)
    return pl.pallas_call(
        digest_kernel,
        grid_spec=pltpu.PrefetchScalarGridSpec(
            num_scalar_prefetch=1,
            grid=(count,),
            in_specs=[whole, square, square, square],
            out_specs=whole,
            scratch_shapes=[pltpu.VMEM((rows, LANES), f32)],
        ),
        out_shape=jax.ShapeDtypeStruct((rows, LANES), f32),
        compiler_params=pltpu.CompilerParams(vmem_limit_bytes=44 << 20),
        name="digest",
    )(quarters, received, integrals, ps, rs)


def finish_kernel(index_ref, recv_ref, orb_ref, swap_ref, out_ref, sums_ref, rows_ref, fock_ref):
    chains = sums_ref.shape[0]

    def clear(n, carry):
        sums_ref[:, pl.ds(SPAN * n, SPAN)] = jnp.zeros((chains, SPAN, SUB, LANES), f32)
        return carry

    lax.fori_loop(0, NB, clear, 0)

    def one(e, carry):
        for turn in range(SLOTS // chains):
            for chain in range(chains):
                slot = turn * chains + chain
                at = index_ref[slot, e]
                sums_ref[chain, at] = (
                    sums_ref[chain, at] + recv_ref[e, SUB * slot : SUB * (slot + 1), :]
                )
        return carry

    lax.fori_loop(0, recv_ref.shape[0], one, 0, unroll=4)

    def column(c, carry):
        parts = []
        for b in range(4):
            tiles = pl.ds((4 * c + b) * SPAN, SPAN)
            total = sums_ref[0, tiles]
            for chain in range(1, chains):
                total = total + sums_ref[chain, tiles]
            parts.append((total * (1.0 / SCALE)).astype(bf16).reshape(SPAN * SUB, LANES))
        out = times(jnp.concatenate(parts, axis=1), swap_ref[...])
        for s in range(4):
            rows_ref[pl.ds(s, LANES, stride=4), :] = out[:, LANES * s : LANES * (s + 1)]
        fock_ref[:, pl.ds(pl.multiple_of(c * LANES, LANES), LANES)] = rows_ref[...].astype(bf16)
        return carry

    lax.fori_loop(0, NB // 4, column, 0, unroll=2)
    out_ref[...] = times(fock_ref[...], orb_ref[...])


def finish(index, arrived, orbitals, swap, rows):
    basis, occupied = orbitals.shape
    chains = 3
    whole = pl.BlockSpec(memory_space=pltpu.VMEM)
    return pl.pallas_call(
        finish_kernel,
        in_specs=[pl.BlockSpec(memory_space=pltpu.SMEM), whole, whole, whole],
        out_specs=whole,
        scratch_shapes=[
            pltpu.VMEM((chains, NB * SPAN, SUB, LANES), f32),
            pltpu.VMEM((rows, LANES), f32),
            pltpu.VMEM((rows, basis), bf16),
        ],
        out_shape=jax.ShapeDtypeStruct((rows, occupied), f32),
        compiler_params=pltpu.CompilerParams(vmem_limit_bytes=32 << 20),
        name="finish",
    )(index, arrived, orbitals, swap)


def tile_index(lists, quarter):
    i, j, k, l = (lists[:, :, role] for role in range(4))
    low = quarter * SPAN
    of_i = i // SPAN == quarter
    of_j = j // SPAN == quarter
    of_k = k // SPAN == quarter

    def pick(mask, value):
        return jnp.sum(jnp.where(mask, value, 0), axis=0)

    return jnp.stack(
        [
            pick(of_i, j * SPAN + i - low),
            pick(of_i, k * SPAN + i - low),
            pick(of_j, l * SPAN + j - low),
            pick(of_j, k * SPAN + j - low),
            pick(of_k, l * SPAN + k - low),
            pick(of_i, l * SPAN + i - low),
        ]
    )


def per_device(integrals, quartets, density, orbitals):
    axes = ("quartet", "pert")
    devices = lax.axis_size("quartet") * lax.axis_size("pert")
    myself = lax.axis_index("quartet") * lax.axis_size("pert") + lax.axis_index("pert")
    quarter = myself % QUARTERS

    swap = group_swap()
    flat = jnp.pad(quartets.reshape(1, 1, GROUP * 4), ((0, 0), (0, 0), (0, LANES - GROUP * 4)))
    lists = lax.all_to_all(
        jnp.broadcast_to(flat, (devices, 1, LANES)), axes, split_axis=0, concat_axis=0, tiled=True
    )
    tiles = cut_tiles(density, swap)
    lists = lists.reshape(devices, LANES).T[: GROUP * 4].reshape(GROUP, 4, devices)
    index = tile_index(lists.transpose(0, 2, 1), quarter)

    outgoing = pick_tiles(index, tiles)
    received = lax.all_to_all(outgoing, axes, 0, 0, tiled=True)
    ps, rs = pairings(integrals, swap)
    quarters = (quartets[:, :3] // SPAN).reshape(-1)
    terms = digest(quarters, received.reshape(-1, LANES), integrals, ps, rs)
    leaving = terms.astype(f16).reshape(devices, CHUNK, LANES)
    landed = lax.all_to_all(leaving, axes, 0, 0, tiled=True)
    return finish(index, landed.astype(f32), orbitals, swap, density.shape[0])


def solution(mesh):
    placed = (
        P(("quartet", "pert"), None, None),
        P(("quartet", "pert"), None),
        P(("quartet", "pert"), None),
        P(),
    )
    return jax.shard_map(
        per_device,
        mesh=mesh,
        in_specs=placed,
        out_specs=P(("quartet", "pert"), None),
        check_vma=False,
    )
```

time: 367 us -> 238 us (0.65)
  waiting for transfers between devices: 124 us -> 36.8 us
  Pallas kernels: 122 us -> 90.6 us
  starting transfers between devices: 10.4 us -> 23.8 us
  between operations: 13.5 us -> 0.1 us
  local copies, waits for them, and re-layouts: 10.2 us -> 3.14 us
    all_gather x1 -> x0, waiting for transfers between devices: 85.5 us -> none  [per_device(): lax.all_gather(jnp.broadcast_to(flat, (SUB, LANES)), axes, axis=0, tiled=...]
    pallas_call x2, Pallas kernels: 55.2 us -> 19.1 us  [the longest x1 11.8 us: finish(): pl.pallas_call(finish_kernel, in_specs=[pl.BlockSpec(memory_space=pltpu.S...]
    all_to_all x0 -> x1, starting transfers between devices: none -> 15.7 us  [per_device(): lax.all_to_all(jnp.broadcast_to(flat, (devices, 1, LANES)), axes, split_a...]
    pallas_call x1, Pallas kernels: 36.3 us -> 44.3 us  [pairings(): pl.pallas_call(pairings_kernel, grid=(count, AREA // LANES), in_specs=[pl...]
    all_to_all x1, waiting for transfers between devices: 38.7 us -> 31.2 us  [per_device(): received = lax.all_to_all(outgoing, axes, 0, 0, tiled=True)]
    unnamed x10 -> x8, local copies, waits for them, and re-layouts: 6.8 us -> 0.87 us
    all_to_all x0 -> x1, waiting for transfers between devices: none -> 5.6 us  [per_device(): lax.all_to_all(jnp.broadcast_to(flat, (devices, 1, LANES)), axes, split_a...]
    pallas_call x1, Pallas kernels: 25 us -> 20.6 us  [digest(): pl.pallas_call(digest_kernel, grid_spec=pltpu.PrefetchScalarGridSpec(num_...]
  transfers between devices with their start and end apart: 2 -> 2, of which waited for: 2 -> 2; matrix products, arithmetic and copies ran while one was open for 0% -> 0% of each run, Pallas kernels for 16% -> 22%
where the time goes in v2:
time: 238 us; the launch traced here: 237 us
  Pallas kernels  90.6 us (38%)
  blocking collectives  81.8 us (34%)
  waiting for transfers between devices  36.8 us (15%)
  starting transfers between devices  23.8 us (10%)
  local copies, waits for them, and re-layouts  3.14 us (1%)
    all_to_all x1, blocking collectives, per_device(): landed = lax.all_to_all(leaving, axes, 0, 0, tiled=True)  81.8 us
    pallas_call x1, Pallas kernels, pairings(): pl.pallas_call(pairings_kernel, grid=(count, AREA // LANES), in_specs=[pl...  44.3 us
    all_to_all x1, waiting for transfers between devices, per_device(): received = lax.all_to_all(outgoing, axes, 0, 0, tiled=True)  31.2 us
    pallas_call x1, Pallas kernels, digest(): pl.pallas_call(digest_kernel, grid_spec=pltpu.PrefetchScalarGridSpec(num_...  20.6 us
    all_to_all x1, starting transfers between devices, per_device(): lax.all_to_all(jnp.broadcast_to(flat, (devices, 1, LANES)), axes, split_a...  15.7 us
    pallas_call x1, Pallas kernels, finish(): pl.pallas_call(finish_kernel, in_specs=[pl.BlockSpec(memory_space=pltpu.S...  11.8 us
    all_to_all x1, starting transfers between devices, per_device(): received = lax.all_to_all(outgoing, axes, 0, 0, tiled=True)  8.12 us
    pallas_call x1, Pallas kernels, cut_tiles(): pl.pallas_call(tiles_kernel, grid=(columns // (width * LANES),), in_specs...  7.3 us
  transfers between devices with their start and end apart: 2, of which 2 were waited for; matrix products, arithmetic and copies ran while one was open for 0% of the time, Pallas kernels for 22%

profile of v2, /device:TPU:1, one launch (start us, length us, event | category | flops | bytes accessed | tf_op | source)
XLA Modules:
  0.0 237.2 jit_solution(2627845863122802360)
XLA Ops:
  0.0 0.8 reshape.22
  0.8 0.7 broadcast_in_dim.15
  1.5 15.7 %all-to-all-start = ((s32[256,1,128]{2,1,0:T(1,128)}), s32[256,1,128]{2,1,0:T(1,128)S(1)}, u32[]{:S(2)}, u32[]{:S(2)}) async-start(s32[256,1,128]{2,1,0:T(1,128)} %broadcast_in_dim.15), calls=%async_computation | async-start | bytes 262144 | tf_op jit(solution)/shard_map/all_to_all | solution.py:326
  17.2 7.3 %cut_tiles.1.tiles_ref = f32[1024,8,128]{2,1,0:T(8,128)} custom-call(bf16[512,2048]{1,0:T(8,128)(2,1)} %dens_ref.1, bf16[512,512]{1,0:T(8,128)(2,1)} %constant.65.clone.swap_ref), custom_call_target="tpu_custom_call" | custom-call | flops 4000000000 | bytes 6291456 | tf_op jit(solution)/shard_map/cut_tiles/pallas_call | solution.py:61
  24.5 5.6 %all-to-all-done = s32[256,1,128]{2,1,0:T(1,128)S(1)} async-done(((s32[256,1,128]{2,1,0:T(1,128)}), s32[256,1,128]{2,1,0:T(1,128)S(1)}, u32[]{:S(2)}, u32[]{:S(2)}) %all-to-all-start) | async-done | bytes 131104 | tf_op jit(solution)/shard_map/all_to_all | solution.py:326
  30.1 0.1 copy.11
  30.2 0.1 fusion.14
  30.2 0.6 stack.27.index_ref
  30.9 6.6 %pick_tiles.1 = bf16[256,48,128]{2,1,0:T(8,128)(2,1)} custom-call(s32[6,256]{1,0:T(8,128)} %stack.27.index_ref, f32[1024,8,128]{2,1,0:T(8,128)} %cut_tiles.1.tiles_ref), custom_call_target="tpu_custom_call" | custom-call | tf_op jit(solution)/shard_map/pick_tiles/pallas_call | solution.py:96
  37.5 0.0 copy-start.3
  37.5 8.1 %all-to-all-start.1 = ((bf16[256,48,128]{2,1,0:T(8,128)(2,1)}), bf16[256,48,128]{2,1,0:T(8,128)(2,1)S(1)}, u32[]{:S(2)}, u32[]{:S(2)}) async-start(bf16[256,48,128]{2,1,0:T(8,128)(2,1)} %pick_tiles.1), calls=%async_computation.1 | async-start | bytes 6291456 | tf_op jit(solution)/shard_map/all_to_all | solution.py:334
  45.6 0.0 copy-done.3
  45.6 0.1 reshape.25.quarter_ref
  45.7 44.3 %pairings.1 = (bf16[4,1024,1024]{2,1,0:T(8,128)(2,1)}, bf16[4,1024,1024]{2,1,0:T(8,128)(2,1)}) custom-call(bf16[4,1024,1024]{2,1,0:T(8,128)(2,1)} %g_ref.3, bf16[512,512]{1,0:T(8,128)(2,1)} %constant.65.clone.swap_ref), custom_call_target="tpu_custom_call" | custom-call | flops 40000000000 | bytes 25165824 | tf_op jit(solution)/shard_map/pairings/pallas_call | solution.py:155
  90.0 31.2 %all-to-all-done.1 = bf16[256,48,128]{2,1,0:T(8,128)(2,1)S(1)} async-done(((bf16[256,48,128]{2,1,0:T(8,128)(2,1)}), bf16[256,48,128]{2,1,0:T(8,128)(2,1)S(1)}, u32[]{:S(2)}, u32[]{:S(2)}) %all-to-all-start.1) | async-done | bytes 3145760 | tf_op jit(solution)/shard_map/all_to_all | solution.py:334
  121.2 20.6 %digest.1 = f32[12288,128]{1,0:T(8,128)S(1)} custom-call(s32[12]{0:T(128)S(1)} %reshape.25.quarter_ref, bf16[12288,128]{1,0:T(8,128)(2,1)S(1)} %bitcast.85, bf16[4,1024,1024]{2,1,0:T(8,128)(2,1)} %g_ref.3, bf16[4,1024,1024]{2,1,0:T(8,128)(2,1)} %get-tuple-element.7.ps_ref, bf16[4,1024,1024]{2,1,0:T(8,128)(2,1)} %get-tuple-element.8.rs_ref), custom_call_target="tpu_custom_call" | custom-call | tf_op jit(solution)/shard_map/digest/pallas_call | solution.py:223
  141.8 0.5 convert_element_type.6
  142.3 81.8 %all_to_all.15 = f16[256,48,128]{2,1,0:T(8,128)(2,1)S(1)} all-to-all(f16[256,48,128]{2,1,0:T(8,128)(2,1)S(1)} %bitcast.86), channel_id=1, replica_groups=mesh['quartet'=128,'pert'=2] {'quartet','pert'}, dimensions={0} | all-to-all | bytes 6291456 | tf_op jit(solution)/shard_map/all_to_all | solution.py:339
  224.1 0.0 copy-start
  224.1 0.5 convert_element_type.7.recv_ref
  224.6 0.7 copy-done
  225.3 0.1 copy-done.1
  225.4 0.0 copy-done.2
  225.4 11.8 %finish.1 = f32[512,256]{1,0:T(8,128)} custom-call(s32[6,256]{1,0:T(8,128)S(1)} %copy-done.2, f32[256,48,128]{2,1,0:T(8,128)S(1)} %convert_element_type.7.recv_ref, bf16[2048,256]{1,0:T(8,128)(2,1)S(1)} %copy-done, bf16[512,512]{1,0:T(8,128)(2,1)S(1)} %copy-done.1), custom_call_target="tpu_custom_call" | custom-call | tf_op jit(solution)/shard_map/finish/pallas_call | solution.py:281
  (6 shorter events, 0.1 us)
Async XLA Ops:
  1.5 28.6 %all-to-all-start = ((s32[256,1,128]{2,1,0:T(1,128)}), s32[256,1,128]{2,1,0:T(1,128)S(1)}, u32[]{:S(2)}, u32[]{:S(2)}) async-start(s32[256,1,128]{2,1,0:T(1,128)} %broadcast_in_dim.15), calls=%async_computation | async-start | bytes 262144 | tf_op jit(solution)/shard_map/all_to_all | solution.py:326
  37.5 8.1 %copy-start.3 = (s32[4,4]{1,0:T(4,128)S(1)}, s32[4,4]{1,0:T(4,128)}, u32[]{:S(2)}) copy-start(s32[4,4]{1,0:T(4,128)} %param.6) | copy-start | bytes 196
  37.5 83.7 %all-to-all-start.1 = ((bf16[256,48,128]{2,1,0:T(8,128)(2,1)}), bf16[256,48,128]{2,1,0:T(8,128)(2,1)S(1)}, u32[]{:S(2)}, u32[]{:S(2)}) async-start(bf16[256,48,128]{2,1,0:T(8,128)(2,1)} %pick_tiles.1), calls=%async_computation.1 | async-start | bytes 6291456 | tf_op jit(solution)/shard_map/all_to_all | solution.py:334
  224.1 1.2 copy-start
  224.1 1.4 copy-start.1
  224.1 1.4 copy-start.2

commit v3 on v2

--- a/solution.py
+++ b/solution.py
@@ -19,6 +19,12 @@
 CHUNK = SLOTS * SUB
 SCALE = 32.0
 
+MESH = pl.DeviceIdType.MESH
+SPREAD_VMEM = 57 << 20
+PICK_VMEM = 58 << 20
+PAIRINGS_VMEM = 56 << 20
+DIGEST_VMEM = 44 << 20
+
 f32 = jnp.float32
 bf16 = jnp.bfloat16
 f16 = jnp.float16
@@ -37,42 +43,122 @@
     return lax.dot_general(left, right, (((1,), (1,)), ((), ())), preferred_element_type=f32)
 
 
-def tiles_kernel(dens_ref, swap_ref, tiles_ref, rows_ref):
-    width = dens_ref.shape[1] // LANES
-    parts = []
-    for n in range(width):
-        rows_ref[n] = dens_ref[:, LANES * n : LANES * (n + 1)].astype(f32)
-        parts.append(
-            jnp.concatenate(
-                [rows_ref[n, pl.ds(s, LANES, stride=4), :].astype(bf16) for s in range(4)], axis=1
+def spread_kernel(
+    list_ref,
+    dens_from,
+    swap_from,
+    lists_ref,
+    tiles_to,
+    tiles_ref,
+    rows_ref,
+    dens_ref,
+    swap_ref,
+    send_sem,
+    recv_sem,
+    own_sem,
+    store_sem,
+):
+    chip, core = lax.axis_index("quartet"), lax.axis_index("pert")
+    x, y, z = chip % 4, (chip // 4) % 4, chip // 16
+    steps = (
+        (2 * chip + core, 1, [(chip, (core + 1) % 2)]),
+        (2 * chip, 2, [(chip - x + (x + n) % 4, core) for n in range(1, 4)]),
+        (8 * (chip // 4), 8, [(chip - 4 * y + 4 * ((y + n) % 4), core) for n in range(1, 4)]),
+        (32 * z, 32, [(chip - 16 * z + 16 * ((z + n) % 8), core) for n in range(1, 8)]),
+    )
+    barrier = pltpu.get_barrier_semaphore()
+    for _, _, partners in steps:
+        for partner in partners:
+            pl.semaphore_signal(barrier, inc=1, device_id=partner, device_id_type=MESH)
+    own = pltpu.make_async_copy(list_ref, lists_ref.at[pl.ds(2 * chip + core, 1)], own_sem.at[0])
+    own.start()
+    fetches = (
+        pltpu.make_async_copy(dens_from, dens_ref, own_sem.at[1]),
+        pltpu.make_async_copy(swap_from, swap_ref, own_sem.at[2]),
+    )
+    for fetch in fetches:
+        fetch.start()
+
+    wide = rows_ref.shape[0]
+
+    def cut(n):
+        parts = []
+        for w in range(wide):
+            columns = slice(LANES * (wide * n + w), LANES * (wide * n + w + 1))
+            rows_ref[w] = dens_ref[:, columns].astype(f32)
+            parts.append(
+                jnp.concatenate(
+                    [rows_ref[w, pl.ds(s, LANES, stride=4), :].astype(bf16) for s in range(4)],
+                    axis=1,
+                )
             )
+        out = times(jnp.concatenate(parts, axis=0), swap_ref[...])
+        for w in range(wide):
+            for b in range(4):
+                first = (4 * (wide * n + w) + b) * SPAN
+                tiles_ref[first : first + SPAN] = out[
+                    LANES * w : LANES * (w + 1), LANES * b : LANES * (b + 1)
+                ].reshape(SPAN, SUB, LANES)
+
+    own.wait()
+    pl.semaphore_wait(barrier, sum(len(partners) for _, _, partners in steps))
+    stores = []
+    for n, (first, count, partners) in enumerate(steps):
+        block = lists_ref.at[pl.ds(first, count)]
+        for partner in partners:
+            pltpu.make_async_remote_copy(
+                src_ref=block,
+                dst_ref=block,
+                send_sem=send_sem.at[n],
+                recv_sem=recv_sem.at[n],
+                device_id=partner,
+                device_id_type=MESH,
+            ).start()
+        if n == 0:
+            for fetch in fetches:
+                fetch.wait()
+        cut(n)
+        part = pl.ds(n * wide * 4 * SPAN, wide * 4 * SPAN)
+        stores.append(
+            pltpu.make_async_copy(tiles_ref.at[part], tiles_to.at[part], store_sem.at[n])
         )
-    out = times(jnp.concatenate(parts, axis=0), swap_ref[...])
-    for n in range(width):
-        for b in range(4):
-            tiles_ref[(4 * n + b) * SPAN : (4 * n + b + 1) * SPAN] = out[
-                LANES * n : LANES * (n + 1), LANES * b : LANES * (b + 1)
-            ].reshape(SPAN, SUB, LANES)
-
-
-def cut_tiles(density, swap):
+        stores[n].start()
+        bytes_in = lists_ref.at[pl.ds(0, count * len(partners))]
+        pltpu.make_async_copy(bytes_in, bytes_in, recv_sem.at[n]).wait()
+    for n, (_, count, partners) in enumerate(steps):
+        bytes_out = lists_ref.at[pl.ds(0, count * len(partners))]
+        pltpu.make_async_copy(bytes_out, bytes_out, send_sem.at[n]).wait()
+        stores[n].wait()
+
+
+def spread_and_cut(own_list, density, swap, devices):
     rows, columns = density.shape
-    width = 2
+    wide = columns // LANES // 4
+    whole = pl.BlockSpec(memory_space=pltpu.VMEM)
+    far = pl.BlockSpec(memory_space=pl.ANY)
     return pl.pallas_call(
-        tiles_kernel,
-        grid=(columns // (width * LANES),),
-        in_specs=[
-            pl.BlockSpec((rows, width * LANES), lambda i: (0, i)),
-            pl.BlockSpec(swap.shape, lambda i: (0, 0)),
-        ],
-        out_specs=pl.BlockSpec((width * 4 * SPAN, SUB, LANES), lambda i: (i, 0, 0)),
-        out_shape=jax.ShapeDtypeStruct((NB * SPAN, SUB, LANES), f32),
-        scratch_shapes=[pltpu.VMEM((width, rows, LANES), f32)],
-        cost_estimate=pl.CostEstimate(
-            flops=4_000_000_000, bytes_accessed=6 * rows * columns, transcendentals=0
+        spread_kernel,
+        in_specs=[whole, far, far],
+        out_specs=[whole, far],
+        out_shape=[
+            jax.ShapeDtypeStruct((devices, 1, LANES), jnp.int32),
+            jax.ShapeDtypeStruct((NB * SPAN, SUB, LANES), f32),
+        ],
+        scratch_shapes=[
+            pltpu.VMEM((NB * SPAN, SUB, LANES), f32),
+            pltpu.VMEM((wide, rows, LANES), f32),
+            pltpu.VMEM(density.shape, bf16),
+            pltpu.VMEM(swap.shape, bf16),
+            pltpu.SemaphoreType.DMA((4,)),
+            pltpu.SemaphoreType.DMA((4,)),
+            pltpu.SemaphoreType.DMA((3,)),
+            pltpu.SemaphoreType.DMA((4,)),
+        ],
+        compiler_params=pltpu.CompilerParams(
+            collective_id=0, has_side_effects=True, vmem_limit_bytes=SPREAD_VMEM
         ),
-        name="cut_tiles",
-    )(density, swap)
+        name="spread_and_cut",
+    )(own_list, density, swap)
 
 
 def pick_kernel(index_ref, tiles_ref, out_ref):
@@ -102,7 +188,7 @@
             out_specs=pl.BlockSpec((per_step, CHUNK, LANES), lambda i, index: (i, 0, 0)),
         ),
         out_shape=jax.ShapeDtypeStruct((devices, CHUNK, LANES), bf16),
-        compiler_params=pltpu.CompilerParams(vmem_limit_bytes=58 << 20),
+        compiler_params=pltpu.CompilerParams(vmem_limit_bytes=PICK_VMEM),
         name="pick_tiles",
     )(index, tiles)
 
@@ -163,7 +249,7 @@
         out_shape=[shape, shape],
         scratch_shapes=[pltpu.VMEM((AREA, LANES), f32)]
         + [pltpu.VMEM((AREA // LANES, AREA, LANES), f32)] * 2,
-        compiler_params=pltpu.CompilerParams(vmem_limit_bytes=56 << 20),
+        compiler_params=pltpu.CompilerParams(vmem_limit_bytes=PAIRINGS_VMEM),
         cost_estimate=pl.CostEstimate(
             flops=40_000_000_000, bytes_accessed=3 * 2 * count * AREA * AREA, transcendentals=0
         ),
@@ -171,22 +257,27 @@
     )(integrals, swap)
 
 
-def digest_kernel(quarter_ref, recv_ref, g_ref, ps_ref, rs_ref, out_ref, rows_ref):
-    m = pl.program_id(0)
-
-    @pl.when(m == 0)
-    def _():
-        def widen(x, carry):
-            at = pl.multiple_of(x * QUARTERS * CHUNK, QUARTERS * CHUNK)
-            rows_ref[pl.ds(at, QUARTERS * CHUNK), :] = recv_ref[
-                pl.ds(at, QUARTERS * CHUNK), :
-            ].astype(f32)
-            return carry
-
-        lax.fori_loop(0, P_SIZE, widen, 0)
-
-    stride = QUARTERS * CHUNK
-    q_i, q_j, q_k = (quarter_ref[3 * m + role] for role in range(3))
+def digest_kernel(
+    quarter_ref, recv_ref, g_ref, ps_ref, rs_ref, out_ref, rows_ref, made_ref, square_ref, sem
+):
+    count = g_ref.shape[0]
+    slots = square_ref.shape[0]
+    message = QUARTERS * CHUNK
+    stride = message + 1
+    squares = [ref.at[m] for m in range(count) for ref in (g_ref, ps_ref, rs_ref)]
+    loads = [
+        pltpu.make_async_copy(square, square_ref.at[n % slots], sem.at[n % slots])
+        for n, square in enumerate(squares)
+    ]
+    for load in loads[: slots - 1]:
+        load.start()
+
+    def widen(x, carry):
+        at = pl.multiple_of(x * message, message)
+        rows_ref[pl.ds(x * stride, message), :] = recv_ref[pl.ds(at, message), :].astype(f32)
+        return carry
+
+    lax.fori_loop(0, P_SIZE, widen, 0)
 
     def fetch(quarter, slot):
         first = quarter * CHUNK + slot * SUB
@@ -201,36 +292,53 @@
     def put(quarter, slot, value):
         first = quarter * CHUNK + slot * SUB
         for c in range(SUB):
-            out_ref[pl.ds(first + c, P_SIZE, stride=stride), :] = value[
+            made_ref[pl.ds(first + c, P_SIZE, stride=stride), :] = value[
                 :, LANES * c : LANES * (c + 1)
             ]
 
-    g, ps, rs = g_ref[0], ps_ref[0], rs_ref[0]
     half = -0.5 * SCALE
-    put(q_i, 0, SCALE * times_turned(fetch(q_k, 4), g))
-    put(q_k, 4, SCALE * times(fetch(q_i, 0), g))
-    put(q_i, 1, half * times_turned(fetch(q_j, 2), ps))
-    put(q_j, 2, half * times(fetch(q_i, 1), ps))
-    put(q_i, 5, half * times(fetch(q_j, 3), rs))
-    put(q_j, 3, half * times_turned(fetch(q_i, 5), rs))
+    for n, load in enumerate(loads):
+        q_i, q_j, q_k = (quarter_ref[3 * (n // 3) + role] for role in range(3))
+        load.wait()
+        if n + slots - 1 < len(loads):
+            loads[n + slots - 1].start()
+        square = square_ref[n % slots]
+        if n % 3 == 0:
+            put(q_i, 0, SCALE * times_turned(fetch(q_k, 4), square))
+            put(q_k, 4, SCALE * times(fetch(q_i, 0), square))
+        elif n % 3 == 1:
+            put(q_i, 1, half * times_turned(fetch(q_j, 2), square))
+            put(q_j, 2, half * times(fetch(q_i, 1), square))
+        else:
+            put(q_i, 5, half * times(fetch(q_j, 3), square))
+            put(q_j, 3, half * times_turned(fetch(q_i, 5), square))
+
+    def close_up(x, carry):
+        at = pl.multiple_of(x * message, message)
+        out_ref[pl.ds(at, message), :] = made_ref[pl.ds(x * stride, message), :]
+        return carry
+
+    lax.fori_loop(0, P_SIZE, close_up, 0)
 
 
 def digest(quarters, received, integrals, ps, rs):
-    count = integrals.shape[0]
     rows = received.shape[0]
-    square = pl.BlockSpec((1, AREA, AREA), lambda m, q: (m, 0, 0))
+    slots = 4
     whole = pl.BlockSpec(memory_space=pltpu.VMEM)
+    far = pl.BlockSpec(memory_space=pl.ANY)
+    spaced = pltpu.VMEM((rows + P_SIZE, LANES), f32)
     return pl.pallas_call(
         digest_kernel,
-        grid_spec=pltpu.PrefetchScalarGridSpec(
-            num_scalar_prefetch=1,
-            grid=(count,),
-            in_specs=[whole, square, square, square],
-            out_specs=whole,
-            scratch_shapes=[pltpu.VMEM((rows, LANES), f32)],
-        ),
+        in_specs=[pl.BlockSpec(memory_space=pltpu.SMEM), whole, far, far, far],
+        out_specs=whole,
+        scratch_shapes=[
+            spaced,
+            spaced,
+            pltpu.VMEM((slots, AREA, AREA), bf16),
+            pltpu.SemaphoreType.DMA((slots,)),
+        ],
         out_shape=jax.ShapeDtypeStruct((rows, LANES), f32),
-        compiler_params=pltpu.CompilerParams(vmem_limit_bytes=44 << 20),
+        compiler_params=pltpu.CompilerParams(vmem_limit_bytes=DIGEST_VMEM),
         name="digest",
     )(quarters, received, integrals, ps, rs)
 
@@ -246,31 +354,42 @@
 
     def one(e, carry):
         for turn in range(SLOTS // chains):
+            slots = range(turn * chains, (turn + 1) * chains)
+            at = [index_ref[slot, e] for slot in slots]
+            new = [
+                sums_ref[chain, at[chain]] + recv_ref[e, SUB * slot : SUB * (slot + 1), :]
+                for chain, slot in enumerate(slots)
+            ]
             for chain in range(chains):
-                slot = turn * chains + chain
-                at = index_ref[slot, e]
-                sums_ref[chain, at] = (
-                    sums_ref[chain, at] + recv_ref[e, SUB * slot : SUB * (slot + 1), :]
-                )
+                sums_ref[chain, at[chain]] = new[chain]
         return carry
 
     lax.fori_loop(0, recv_ref.shape[0], one, 0, unroll=4)
 
-    def column(c, carry):
-        parts = []
-        for b in range(4):
-            tiles = pl.ds((4 * c + b) * SPAN, SPAN)
-            total = sums_ref[0, tiles]
-            for chain in range(1, chains):
-                total = total + sums_ref[chain, tiles]
-            parts.append((total * (1.0 / SCALE)).astype(bf16).reshape(SPAN * SUB, LANES))
-        out = times(jnp.concatenate(parts, axis=1), swap_ref[...])
-        for s in range(4):
-            rows_ref[pl.ds(s, LANES, stride=4), :] = out[:, LANES * s : LANES * (s + 1)]
-        fock_ref[:, pl.ds(pl.multiple_of(c * LANES, LANES), LANES)] = rows_ref[...].astype(bf16)
-        return carry
-
-    lax.fori_loop(0, NB // 4, column, 0, unroll=2)
+    wide = rows_ref.shape[0]
+
+    def columns(c, carry):
+        lefts = []
+        for w in range(wide):
+            parts = []
+            for b in range(4):
+                tiles = pl.ds((4 * (wide * c + w) + b) * SPAN, SPAN)
+                total = sums_ref[0, tiles]
+                for chain in range(1, chains):
+                    total = total + sums_ref[chain, tiles]
+                parts.append((total * (1.0 / SCALE)).astype(bf16).reshape(SPAN * SUB, LANES))
+            lefts.append(jnp.concatenate(parts, axis=1))
+        out = times(jnp.concatenate(lefts, axis=0), swap_ref[...])
+        for w in range(wide):
+            for s in range(4):
+                rows_ref[w, pl.ds(s, LANES, stride=4), :] = out[
+                    LANES * w : LANES * (w + 1), LANES * s : LANES * (s + 1)
+                ]
+            at = pl.multiple_of((wide * c + w) * LANES, LANES)
+            fock_ref[:, pl.ds(at, LANES)] = rows_ref[w].astype(bf16)
+        return carry
+
+    lax.fori_loop(0, NB // 4 // wide, columns, 0)
     out_ref[...] = times(fock_ref[...], orb_ref[...])
 
 
@@ -284,7 +403,7 @@
         out_specs=whole,
         scratch_shapes=[
             pltpu.VMEM((chains, NB * SPAN, SUB, LANES), f32),
-            pltpu.VMEM((rows, LANES), f32),
+            pltpu.VMEM((4, rows, LANES), f32),
             pltpu.VMEM((rows, basis), bf16),
         ],
         out_shape=jax.ShapeDtypeStruct((rows, occupied), f32),
@@ -323,10 +442,7 @@
 
     swap = group_swap()
     flat = jnp.pad(quartets.reshape(1, 1, GROUP * 4), ((0, 0), (0, 0), (0, LANES - GROUP * 4)))
-    lists = lax.all_to_all(
-        jnp.broadcast_to(flat, (devices, 1, LANES)), axes, split_axis=0, concat_axis=0, tiled=True
-    )
-    tiles = cut_tiles(density, swap)
+    lists, tiles = spread_and_cut(flat, density, swap, devices)
     lists = lists.reshape(devices, LANES).T[: GROUP * 4].reshape(GROUP, 4, devices)
     index = tile_index(lists.transpose(0, 2, 1), quarter)
 

time: 238 us -> 226 us (0.950)
  starting transfers between devices: 23.8 us -> 10.5 us
  Pallas kernels: 90.6 us -> 97.3 us
  waiting for transfers between devices: 36.8 us -> 31.2 us
    all_to_all x1 -> x0, starting transfers between devices: 15.7 us -> none  [per_device(): lax.all_to_all(jnp.broadcast_to(flat, (devices, 1, LANES)), axes, split_a...]
    pallas_call x2, Pallas kernels: 27.9 us -> 38.1 us  [the longest x1 21.8 us: spread_and_cut(): pl.pallas_call(spread_kernel, in_specs=[whole, far, far], out_specs=[whol...]
    all_to_all x1 -> x0, waiting for transfers between devices: 5.6 us -> none  [per_device(): lax.all_to_all(jnp.broadcast_to(flat, (devices, 1, LANES)), axes, split_a...]
    pallas_call x1, Pallas kernels: 11.8 us -> 8.32 us  [finish(): pl.pallas_call(finish_kernel, in_specs=[pl.BlockSpec(memory_space=pltpu.S...]
  transfers between devices with their start and end apart: 2 -> 1, of which waited for: 2 -> 1; matrix products, arithmetic and copies ran while one was open for 0% -> 0% of each run, Pallas kernels for 22% -> 20%
where the time goes in v3:
time: 226 us
  Pallas kernels  97.3 us (43%)
  blocking collectives  81.8 us (36%)
  waiting for transfers between devices  31.2 us (14%)
  starting transfers between devices  10.5 us (5%)
  local copies, waits for them, and re-layouts  3.86 us (2%)
    all_to_all x1, blocking collectives, per_device(): landed = lax.all_to_all(leaving, axes, 0, 0, tiled=True)  81.8 us
    pallas_call x1, Pallas kernels, pairings(): pl.pallas_call(pairings_kernel, grid=(count, AREA // LANES), in_specs=[pl...  44.3 us
    all_to_all x1, waiting for transfers between devices, per_device(): received = lax.all_to_all(outgoing, axes, 0, 0, tiled=True)  31.2 us
    pallas_call x1, Pallas kernels, spread_and_cut(): pl.pallas_call(spread_kernel, in_specs=[whole, far, far], out_specs=[whol...  21.8 us
    pallas_call x1, Pallas kernels, digest(): pl.pallas_call(digest_kernel, in_specs=[pl.BlockSpec(memory_space=pltpu.S...  16.3 us
    all_to_all x1, starting transfers between devices, per_device(): received = lax.all_to_all(outgoing, axes, 0, 0, tiled=True)  10.5 us
    pallas_call x1, Pallas kernels, finish(): pl.pallas_call(finish_kernel, in_specs=[pl.BlockSpec(memory_space=pltpu.S...  8.32 us
    pallas_call x1, Pallas kernels, pick_tiles(): pl.pallas_call(pick_kernel, grid_spec=pltpu.PrefetchScalarGridSpec(num_sc...  6.62 us
  transfers between devices with their start and end apart: 1, of which 1 were waited for; matrix products, arithmetic and copies ran while one was open for 0% of the time, Pallas kernels for 20%

profile of v3, /device:TPU:1, one launch (start us, length us, event | category | flops | bytes accessed | tf_op | source)
XLA Modules:
  0.0 225.7 jit_solution(3380970804677342517)
XLA Ops:
  0.0 0.8 reshape.20
  0.8 0.5 pad.4.list_ref
  1.3 21.8 %spread_and_cut.1 = (s32[256,1,128]{2,1,0:T(1,128)}, f32[1024,8,128]{2,1,0:T(8,128)}) custom-call(s32[1,1,128]{2,1,0:T(1,128)} %pad.4.list_ref, bf16[512,2048]{1,0:T(8,128)(2,1)} %dens_from.1, bf16[512,512]{1,0:T(8,128)(2,1)} %constant.65.clone.swap_from.swap_ref), custom_call_target="tpu_custom_call" | custom-call | tf_op jit(solution)/shard_map/spread_and_cut/pallas_call | solution.py:139
  23.1 1.0 copy.9
  24.1 0.6 stack.27.index_ref
  24.8 6.6 %pick_tiles.1 = bf16[256,48,128]{2,1,0:T(8,128)(2,1)} custom-call(s32[6,256]{1,0:T(8,128)} %stack.27.index_ref, f32[1024,8,128]{2,1,0:T(8,128)} %get-tuple-element.10.tiles_ref), custom_call_target="tpu_custom_call" | custom-call | tf_op jit(solution)/shard_map/pick_tiles/pallas_call | solution.py:182
  31.4 0.0 copy-start.3
  31.4 10.5 %all-to-all-start = ((bf16[256,48,128]{2,1,0:T(8,128)(2,1)}), bf16[256,48,128]{2,1,0:T(8,128)(2,1)S(1)}, u32[]{:S(2)}, u32[]{:S(2)}) async-start(bf16[256,48,128]{2,1,0:T(8,128)(2,1)} %pick_tiles.1), calls=%async_computation | async-start | bytes 6291456 | tf_op jit(solution)/shard_map/all_to_all | solution.py:450
  41.9 0.0 copy-done.3
  41.9 0.1 reshape.23.quarter_ref
  42.0 44.3 %pairings.1 = (bf16[4,1024,1024]{2,1,0:T(8,128)(2,1)}, bf16[4,1024,1024]{2,1,0:T(8,128)(2,1)}) custom-call(bf16[4,1024,1024]{2,1,0:T(8,128)(2,1)} %g_ref.3, bf16[512,512]{1,0:T(8,128)(2,1)} %constant.65.clone.swap_from.swap_ref), custom_call_target="tpu_custom_call" | custom-call | flops 40000000000 | bytes 25165824 | tf_op jit(solution)/shard_map/pairings/pallas_call | solution.py:241
  86.2 31.2 %all-to-all-done = bf16[256,48,128]{2,1,0:T(8,128)(2,1)S(1)} async-done(((bf16[256,48,128]{2,1,0:T(8,128)(2,1)}), bf16[256,48,128]{2,1,0:T(8,128)(2,1)S(1)}, u32[]{:S(2)}, u32[]{:S(2)}) %all-to-all-start) | async-done | bytes 3145760 | tf_op jit(solution)/shard_map/all_to_all | solution.py:450
  117.4 16.3 %digest.1 = f32[12288,128]{1,0:T(8,128)S(1)} custom-call(s32[12]{0:T(128)S(1)} %reshape.23.quarter_ref, bf16[12288,128]{1,0:T(8,128)(2,1)S(1)} %bitcast.83, bf16[4,1024,1024]{2,1,0:T(8,128)(2,1)} %g_ref.3, bf16[4,1024,1024]{2,1,0:T(8,128)(2,1)} %get-tuple-element.11.ps_ref, bf16[4,1024,1024]{2,1,0:T(8,128)(2,1)} %get-tuple-element.12.rs_ref), custom_call_target="tpu_custom_call" | custom-call | tf_op jit(solution)/shard_map/digest/pallas_call | solution.py:330
  133.7 0.5 convert_element_type.6
  134.2 81.8 %all_to_all.10 = f16[256,48,128]{2,1,0:T(8,128)(2,1)S(1)} all-to-all(f16[256,48,128]{2,1,0:T(8,128)(2,1)S(1)} %bitcast.84), channel_id=1, replica_groups=mesh['quartet'=128,'pert'=2] {'quartet','pert'}, dimensions={0} | all-to-all | bytes 6291456 | tf_op jit(solution)/shard_map/all_to_all | solution.py:455
  216.0 0.0 copy-start
  216.0 0.0 copy-start.1
  216.0 0.0 copy-start.2
  216.0 0.5 convert_element_type.7.recv_ref
  216.5 0.5 copy-done
  217.0 0.3 copy-done.1
  217.4 0.0 copy-done.2
  217.4 8.3 %finish.1 = f32[512,256]{1,0:T(8,128)} custom-call(s32[6,256]{1,0:T(8,128)S(1)} %copy-done.2, f32[256,48,128]{2,1,0:T(8,128)S(1)} %convert_element_type.7.recv_ref, bf16[2048,256]{1,0:T(8,128)(2,1)S(1)} %copy-done.1, bf16[512,512]{1,0:T(8,128)(2,1)S(1)} %copy-done), custom_call_target="tpu_custom_call" | custom-call | tf_op jit(solution)/shard_map/finish/pallas_call | solution.py:400
  (4 shorter events, 0.1 us)
Async XLA Ops:
  31.4 10.5 %copy-start.3 = (s32[4,4]{1,0:T(4,128)S(1)}, s32[4,4]{1,0:T(4,128)}, u32[]{:S(2)}) copy-start(s32[4,4]{1,0:T(4,128)} %param.6) | copy-start | bytes 196
  31.4 86.1 %all-to-all-start = ((bf16[256,48,128]{2,1,0:T(8,128)(2,1)}), bf16[256,48,128]{2,1,0:T(8,128)(2,1)S(1)}, u32[]{:S(2)}, u32[]{:S(2)}) async-start(bf16[256,48,128]{2,1,0:T(8,128)(2,1)} %pick_tiles.1), calls=%async_computation | async-start | bytes 6291456 | tf_op jit(solution)/shard_map/all_to_all | solution.py:450
  216.0 1.0 copy-start
  216.0 1.4 copy-start.1
  216.0 1.4 copy-start.2

commit v4 on v3

v4 whole, which is shorter than its diff:
```python
import jax
import jax.numpy as jnp
import numpy as np
from jax import lax
from jax.experimental import pallas as pl
from jax.experimental.pallas import tpu as pltpu
from jax.sharding import PartitionSpec as P

P_SIZE = 64
S = 32
NB = 64
QUARTERS = 4
SPAN = NB // QUARTERS
GROUP = 4
SLOTS = 6
TILES = ((0, 1), (0, 2), (1, 3), (1, 2), (2, 3), (0, 3))
LANES = 128
SUB = 8
AREA = S * S
CHUNK = SLOTS * SUB
SCALE = 32.0

MESH = pl.DeviceIdType.MESH
EXCHANGE_VMEM = 46 << 20
DIGEST_VMEM = 44 << 20

f32 = jnp.float32
bf16 = jnp.bfloat16
f16 = jnp.float16


def group_swap():
    eye = np.eye(4 * LANES, dtype=np.float32)
    return jnp.asarray(eye.reshape(4, 4, S, 4 * LANES).transpose(1, 0, 2, 3).reshape(eye.shape), bf16)


def times(left, right):
    return jnp.dot(left, right, preferred_element_type=f32)


def times_turned(left, right):
    return lax.dot_general(left, right, (((1,), (1,)), ((), ())), preferred_element_type=f32)


def own_indices(quartet_ref, row_ref):
    members = [[quartet_ref[m, role] for role in range(4)] for m in range(GROUP)]
    for quarter in range(QUARTERS):
        low = quarter * SPAN

        def pick(row, column):
            total = jnp.int32(0)
            for member in members:
                within = jnp.logical_and(member[row] >= low, member[row] < low + SPAN)
                value = member[column] * SPAN + member[row] - low
                total = total + jnp.where(within, value, 0)
            return total

        for slot, (row, column) in enumerate(TILES):
            row_ref[0, 0, quarter * SLOTS + slot] = pick(row, column)
    for lane in range(QUARTERS * SLOTS, LANES):
        row_ref[0, 0, lane] = jnp.int32(0)


def exchange_kernel(
    quartet_ref,
    dens_from,
    swap_from,
    g_from,
    slots_ref,
    received_ref,
    ps_to,
    rs_to,
    row_ref,
    index_ref,
    lists_ref,
    tiles_ref,
    rows_ref,
    dens_ref,
    swap_ref,
    message_ref,
    g_ref,
    strip_ref,
    ps_rows,
    rs_rows,
    ps_ref,
    rs_ref,
    step_send,
    step_recv,
    own_sem,
    send_sem,
    recv_sem,
    g_sem,
    pair_sem,
):
    chip, core = lax.axis_index("quartet"), lax.axis_index("pert")
    x, y, z = chip % 4, (chip // 4) % 4, chip // 16
    me = 2 * chip + core
    devices = lists_ref.shape[0]

    steps = (
        (me, 1, [(chip, (core + 1) % 2)]),
        (2 * chip, 2, [(chip - x + (x + n) % 4, core) for n in range(1, 4)]),
        (8 * (chip // 4), 8, [(chip - 4 * y + 4 * ((y + n) % 4), core) for n in range(1, 4)]),
        (32 * z, 32, [(chip - 16 * z + 16 * ((z + n) % 8), core) for n in range(1, 8)]),
    )
    barrier = pltpu.get_barrier_semaphore()
    for _, _, partners in steps:
        for partner in partners:
            pl.semaphore_signal(barrier, inc=1, device_id=partner, device_id_type=MESH)
    fetches = (
        pltpu.make_async_copy(dens_from, dens_ref, own_sem.at[1]),
        pltpu.make_async_copy(swap_from, swap_ref, own_sem.at[2]),
    )
    for fetch in fetches:
        fetch.start()
    own_indices(quartet_ref, row_ref)
    own = pltpu.make_async_copy(row_ref, lists_ref.at[pl.ds(me, 1)], own_sem.at[0])
    own.start()

    wide = rows_ref.shape[0]

    def cut(n):
        parts = []
        for w in range(wide):
            columns = slice(LANES * (wide * n + w), LANES * (wide * n + w + 1))
            rows_ref[w] = dens_ref[:, columns].astype(f32)
            parts.append(
                jnp.concatenate(
                    [rows_ref[w, pl.ds(s, LANES, stride=4), :].astype(bf16) for s in range(4)],
                    axis=1,
                )
            )
        out = times(jnp.concatenate(parts, axis=0), swap_ref[...])
        for w in range(wide):
            for b in range(4):
                first = (4 * (wide * n + w) + b) * SPAN
                tiles_ref[first : first + SPAN] = out[
                    LANES * w : LANES * (w + 1), LANES * b : LANES * (b + 1)
                ].reshape(SPAN, SUB, LANES)

    own.wait()
    pl.semaphore_wait(barrier, sum(len(partners) for _, _, partners in steps))
    for n, (first, count, partners) in enumerate(steps):
        block = lists_ref.at[pl.ds(first, count)]
        for partner in partners:
            pltpu.make_async_remote_copy(
                src_ref=block,
                dst_ref=block,
                send_sem=step_send.at[n],
                recv_sem=step_recv.at[n],
                device_id=partner,
                device_id_type=MESH,
            ).start()
        if n == 0:
            for fetch in fetches:
                fetch.wait()
        cut(n)
        bytes_in = lists_ref.at[pl.ds(0, count * len(partners))]
        pltpu.make_async_copy(bytes_in, bytes_in, step_recv.at[n]).wait()

    to_scalars = pltpu.make_async_copy(lists_ref, index_ref, own_sem.at[0])
    to_scalars.start()

    count, area = g_from.shape[0], g_from.shape[1]
    strips = area // LANES

    def g_load(n):
        return pltpu.make_async_copy(
            g_from.at[n // strips, :, pl.ds(pl.multiple_of((n % strips) * LANES, LANES), LANES)],
            g_ref.at[n % 2],
            g_sem.at[n % 2],
        )

    g_load(0).start()
    to_scalars.wait()

    base = (me % QUARTERS) * SLOTS

    def pick(device):
        tiles = [tiles_ref[index_ref[device, 0, base + slot]] for slot in range(SLOTS)]
        for pair in range(SLOTS // 2):
            message_ref[device, 16 * pair : 16 * (pair + 1), :] = jnp.concatenate(
                tiles[2 * pair : 2 * pair + 2], axis=0
            ).astype(bf16)

    def send(n, carry):
        device = (me + n) % devices
        pick(device)
        pltpu.make_async_remote_copy(
            src_ref=message_ref.at[device],
            dst_ref=received_ref.at[me],
            send_sem=send_sem,
            recv_sem=recv_sem,
            device_id=(device // 2, device % 2),
            device_id_type=MESH,
        ).start()
        return carry

    lax.fori_loop(1, devices, send, 0)
    pick(me)
    keep = pltpu.make_async_copy(message_ref.at[me], received_ref.at[me], own_sem.at[1])
    keep.start()

    by_lane = lists_ref[...].reshape(devices, LANES).T
    slots = by_lane[:SLOTS]
    for quarter in range(1, QUARTERS):
        mine = by_lane[quarter * SLOTS : (quarter + 1) * SLOTS]
        slots = jnp.where(me % QUARTERS == quarter, mine, slots)
    slots_ref[...] = slots

    def stores(m):
        return (
            pltpu.make_async_copy(ps_ref, ps_to.at[m], pair_sem.at[0]),
            pltpu.make_async_copy(rs_ref, rs_to.at[m], pair_sem.at[1]),
        )

    def strip(n, carry):
        step = n % strips

        @pl.when(n + 1 < count * strips)
        def _():
            g_load(n + 1).start()

        g_load(n).wait()
        g = g_ref.at[n % 2]
        strip_ref[...] = g[...].astype(f32)
        swap = swap_ref[...]

        def spread(parts, target):
            out = times(jnp.concatenate(parts, axis=1), swap)
            for big in range(8):
                for s in range(4):
                    target[big, pl.ds(4 * step + s, S, stride=S), :] = out[
                        S * big : S * (big + 1), LANES * s : LANES * (s + 1)
                    ]

        spread(
            [
                jnp.concatenate(
                    [strip_ref[pl.ds(4 * big + r, S, stride=S), :] for big in range(8)], axis=0
                ).astype(bf16)
                for r in range(4)
            ],
            ps_rows,
        )
        spread(
            [
                jnp.concatenate(
                    [g[S * (4 * big + p) : S * (4 * big + p + 1), :] for big in range(8)], axis=0
                )
                for p in range(4)
            ],
            rs_rows,
        )

        @pl.when(step == strips - 1)
        def _():
            m = n // strips

            @pl.when(m > 0)
            def _():
                for store in stores(m - 1):
                    store.wait()

            for big in range(8):
                lanes = slice(LANES * big, LANES * (big + 1))
                ps_ref[:, lanes] = ps_rows[big].astype(bf16)
                rs_ref[:, lanes] = rs_rows[big].astype(bf16)
            for store in stores(m):
                store.start()

        return carry

    lax.fori_loop(0, count * strips, strip, 0)
    for store in stores(count - 1):
        store.wait()

    keep.wait()
    others = received_ref.at[pl.ds(0, devices - 1)]
    pltpu.make_async_copy(others, others, recv_sem).wait()
    pltpu.make_async_copy(others, others, send_sem).wait()
    for n, (_, count, partners) in enumerate(steps):
        bytes_out = lists_ref.at[pl.ds(0, count * len(partners))]
        pltpu.make_async_copy(bytes_out, bytes_out, step_send.at[n]).wait()


def exchange(quartets, density, swap, integrals, devices):
    rows, columns = density.shape
    count = integrals.shape[0]
    wide = columns // LANES // 4
    whole = pl.BlockSpec(memory_space=pltpu.VMEM)
    far = pl.BlockSpec(memory_space=pltpu.HBM)
    dma = pltpu.SemaphoreType.DMA
    return pl.pallas_call(
        exchange_kernel,
        in_specs=[pl.BlockSpec(memory_space=pltpu.SMEM), far, far, far],
        out_specs=[whole, whole, far, far],
        out_shape=[
            jax.ShapeDtypeStruct((SLOTS, devices), jnp.int32),
            jax.ShapeDtypeStruct((devices, CHUNK, LANES), bf16),
            jax.ShapeDtypeStruct((count, AREA, AREA), bf16),
            jax.ShapeDtypeStruct((count, AREA, AREA), bf16),
        ],
        scratch_shapes=[
            pltpu.SMEM((1, 1, LANES), jnp.int32),
            pltpu.SMEM((devices, 1, LANES), jnp.int32),
            pltpu.VMEM((devices, 1, LANES), jnp.int32),
            pltpu.VMEM((NB * SPAN, SUB, LANES), f32),
            pltpu.VMEM((wide, rows, LANES), f32),
            pltpu.VMEM(density.shape, bf16),
            pltpu.VMEM(swap.shape, bf16),
            pltpu.VMEM((devices, CHUNK, LANES), bf16),
            pltpu.VMEM((2, AREA, LANES), bf16),
            pltpu.VMEM((AREA, LANES), f32),
            pltpu.VMEM((AREA // LANES, AREA, LANES), f32),
            pltpu.VMEM((AREA // LANES, AREA, LANES), f32),
            pltpu.VMEM((AREA, AREA), bf16),
            pltpu.VMEM((AREA, AREA), bf16),
            dma((4,)),
            dma((4,)),
            dma((3,)),
            dma,
            dma,
            dma((2,)),
            dma((2,)),
        ],
        compiler_params=pltpu.CompilerParams(
            collective_id=0, has_side_effects=True, vmem_limit_bytes=EXCHANGE_VMEM
        ),
        name="exchange",
    )(quartets, density, swap, integrals)


def digest_kernel(
    quartet_ref, recv_ref, g_ref, ps_ref, rs_ref, out_ref, rows_ref, made_ref, square_ref, sem
):
    count = g_ref.shape[0]
    slots = square_ref.shape[0]
    message = QUARTERS * CHUNK
    stride = message + 1
    squares = [ref.at[m] for m in range(count) for ref in (g_ref, ps_ref, rs_ref)]
    loads = [
        pltpu.make_async_copy(square, square_ref.at[n % slots], sem.at[n % slots])
        for n, square in enumerate(squares)
    ]
    for load in loads[: slots - 1]:
        load.start()

    def widen(x, carry):
        at = pl.multiple_of(x * message, message)
        rows_ref[pl.ds(x * stride, message), :] = recv_ref[pl.ds(at, message), :].astype(f32)
        return carry

    lax.fori_loop(0, P_SIZE, widen, 0)

    def fetch(quarter, slot):
        first = quarter * CHUNK + slot * SUB
        return jnp.concatenate(
            [
                rows_ref[pl.ds(first + c, P_SIZE, stride=stride), :].astype(bf16)
                for c in range(SUB)
            ],
            axis=1,
        )

    def put(quarter, slot, value):
        first = quarter * CHUNK + slot * SUB
        for c in range(SUB):
            made_ref[pl.ds(first + c, P_SIZE, stride=stride), :] = value[
                :, LANES * c : LANES * (c + 1)
            ]

    half = -0.5 * SCALE
    for n, load in enumerate(loads):
        q_i, q_j, q_k = (quartet_ref[n // 3, role] // SPAN for role in range(3))
        load.wait()
        if n + slots - 1 < len(loads):
            loads[n + slots - 1].start()
        square = square_ref[n % slots]
        if n % 3 == 0:
            put(q_i, 0, SCALE * times_turned(fetch(q_k, 4), square))
            put(q_k, 4, SCALE * times(fetch(q_i, 0), square))
        elif n % 3 == 1:
            put(q_i, 1, half * times_turned(fetch(q_j, 2), square))
            put(q_j, 2, half * times(fetch(q_i, 1), square))
        else:
            put(q_i, 5, half * times(fetch(q_j, 3), square))
            put(q_j, 3, half * times_turned(fetch(q_i, 5), square))

    def close_up(x, carry):
        at = pl.multiple_of(x * message, message)
        out_ref[pl.ds(at, message), :] = made_ref[pl.ds(x * stride, message), :]
        return carry

    lax.fori_loop(0, P_SIZE, close_up, 0)


def digest(quartets, received, integrals, ps, rs):
    rows = received.shape[0]
    slots = 4
    whole = pl.BlockSpec(memory_space=pltpu.VMEM)
    far = pl.BlockSpec(memory_space=pltpu.HBM)
    spaced = pltpu.VMEM((rows + P_SIZE, LANES), f32)
    return pl.pallas_call(
        digest_kernel,
        in_specs=[pl.BlockSpec(memory_space=pltpu.SMEM), whole, far, far, far],
        out_specs=whole,
        scratch_shapes=[
            spaced,
            spaced,
            pltpu.VMEM((slots, AREA, AREA), bf16),
            pltpu.SemaphoreType.DMA((slots,)),
        ],
        out_shape=jax.ShapeDtypeStruct((rows, LANES), f32),
        compiler_params=pltpu.CompilerParams(vmem_limit_bytes=DIGEST_VMEM),
        name="digest",
    )(quartets, received, integrals, ps, rs)


def finish_kernel(index_ref, recv_ref, orb_ref, swap_ref, out_ref, sums_ref, rows_ref, fock_ref):
    chains = sums_ref.shape[0]

    def clear(n, carry):
        sums_ref[:, pl.ds(SPAN * n, SPAN)] = jnp.zeros((chains, SPAN, SUB, LANES), f32)
        return carry

    lax.fori_loop(0, NB, clear, 0)

    def one(e, carry):
        for turn in range(SLOTS // chains):
            slots = range(turn * chains, (turn + 1) * chains)
            at = [index_ref[slot, e] for slot in slots]
            new = [
                sums_ref[chain, at[chain]] + recv_ref[e, SUB * slot : SUB * (slot + 1), :]
                for chain, slot in enumerate(slots)
            ]
            for chain in range(chains):
                sums_ref[chain, at[chain]] = new[chain]
        return carry

    lax.fori_loop(0, recv_ref.shape[0], one, 0, unroll=4)

    wide = rows_ref.shape[0]

    def columns(c, carry):
        lefts = []
        for w in range(wide):
            parts = []
            for b in range(4):
                tiles = pl.ds((4 * (wide * c + w) + b) * SPAN, SPAN)
                total = sums_ref[0, tiles]
                for chain in range(1, chains):
                    total = total + sums_ref[chain, tiles]
                parts.append((total * (1.0 / SCALE)).astype(bf16).reshape(SPAN * SUB, LANES))
            lefts.append(jnp.concatenate(parts, axis=1))
        out = times(jnp.concatenate(lefts, axis=0), swap_ref[...])
        for w in range(wide):
            for s in range(4):
                rows_ref[w, pl.ds(s, LANES, stride=4), :] = out[
                    LANES * w : LANES * (w + 1), LANES * s : LANES * (s + 1)
                ]
            at = pl.multiple_of((wide * c + w) * LANES, LANES)
            fock_ref[:, pl.ds(at, LANES)] = rows_ref[w].astype(bf16)
        return carry

    lax.fori_loop(0, NB // 4 // wide, columns, 0)
    out_ref[...] = times(fock_ref[...], orb_ref[...])


def finish(index, arrived, orbitals, swap, rows):
    basis, occupied = orbitals.shape
    chains = 3
    whole = pl.BlockSpec(memory_space=pltpu.VMEM)
    return pl.pallas_call(
        finish_kernel,
        in_specs=[pl.BlockSpec(memory_space=pltpu.SMEM), whole, whole, whole],
        out_specs=whole,
        scratch_shapes=[
            pltpu.VMEM((chains, NB * SPAN, SUB, LANES), f32),
            pltpu.VMEM((4, rows, LANES), f32),
            pltpu.VMEM((rows, basis), bf16),
        ],
        out_shape=jax.ShapeDtypeStruct((rows, occupied), f32),
        compiler_params=pltpu.CompilerParams(vmem_limit_bytes=32 << 20),
        name="finish",
    )(index, arrived, orbitals, swap)


def per_device(integrals, quartets, density, orbitals):
    axes = ("quartet", "pert")
    devices = lax.axis_size("quartet") * lax.axis_size("pert")
    swap = group_swap()
    index, received, ps, rs = exchange(quartets, density, swap, integrals, devices)
    terms = digest(quartets, received.reshape(-1, LANES), integrals, ps, rs)
    leaving = terms.astype(f16).reshape(devices, CHUNK, LANES)
    landed = lax.all_to_all(leaving, axes, 0, 0, tiled=True)
    return finish(index, landed.astype(f32), orbitals, swap, density.shape[0])


def solution(mesh):
    placed = (
        P(("quartet", "pert"), None, None),
        P(("quartet", "pert"), None),
        P(("quartet", "pert"), None),
        P(),
    )
    return jax.shard_map(
        per_device,
        mesh=mesh,
        in_specs=placed,
        out_specs=P(("quartet", "pert"), None),
        check_vma=False,
    )
```

time: 226 us -> 215 us (0.951)
  waiting for transfers between devices: 31.2 us -> 0 us
  Pallas kernels: 97.3 us -> 121 us
  starting transfers between devices: 10.5 us -> 0 us
  blocking collectives: 81.8 us -> 88.1 us
    all_to_all x1 -> x0, waiting for transfers between devices: 31.2 us -> none  [per_device(): received = lax.all_to_all(outgoing, axes, 0, 0, tiled=True)]
    pallas_call x3 -> x1, Pallas kernels: 72.7 us -> 96.8 us  [exchange(): pl.pallas_call(exchange_kernel, in_specs=[pl.BlockSpec(memory_space=pltpu...]
    all_to_all x1 -> x0, starting transfers between devices: 10.5 us -> none  [per_device(): received = lax.all_to_all(outgoing, axes, 0, 0, tiled=True)]
    all_to_all x1, blocking collectives: 81.8 us -> 88.1 us  [per_device(): landed = lax.all_to_all(leaving, axes, 0, 0, tiled=True)]
    unnamed x8 -> x10, local copies, waits for them, and re-layouts: 0.9 us -> 4.21 us
  transfers between devices with their start and end apart: 1 -> 0, of which waited for: 1 -> 0; matrix products, arithmetic and copies ran while one was open for 0% -> 0% of each run, Pallas kernels for 20% -> 0%
where the time goes in v4:
time: 215 us
  Pallas kernels  121 us (56%)
  blocking collectives  88.1 us (41%)
  local copies, waits for them, and re-layouts  4.21 us (2%)
    pallas_call x1, Pallas kernels, exchange(): pl.pallas_call(exchange_kernel, in_specs=[pl.BlockSpec(memory_space=pltpu...  96.8 us
    all_to_all x1, blocking collectives, per_device(): landed = lax.all_to_all(leaving, axes, 0, 0, tiled=True)  88.1 us
    pallas_call x1, Pallas kernels, digest(): pl.pallas_call(digest_kernel, in_specs=[pl.BlockSpec(memory_space=pltpu.S...  16.3 us
    pallas_call x1, Pallas kernels, finish(): pl.pallas_call(finish_kernel, in_specs=[pl.BlockSpec(memory_space=pltpu.S...  8.34 us

profile of v4, /device:TPU:1, one launch (start us, length us, event | category | flops | bytes accessed | tf_op | source)
XLA Modules:
  0.0 214.7 jit_solution(13012091783350229446)
XLA Ops:
  0.0 0.0 copy-start
  0.0 1.0 copy-done
  1.0 0.0 copy-start.2
  1.0 1.6 copy-done.2
  2.6 0.0 copy-start.4
  2.6 0.7 copy-done.4
  3.3 96.8 %exchange.1 = (s32[6,256]{1,0:T(8,128)S(1)}, bf16[256,48,128]{2,1,0:T(8,128)(2,1)S(1)}, bf16[4,1024,1024]{2,1,0:T(8,128)(2,1)}, bf16[4,1024,1024]{2,1,0:T(8,128)(2,1)}) custom-call(s32[4,4]{1,0:T(4,128)S(1)} %copy-done.4, bf16[512,2048]{1,0:T(8,128)(2,1)S(1)} %copy-done.2, bf16[512,512]{1,0:T(8,128)(2,1)S(1)} %copy-done, bf16[4,1024,1024]{2,1,0:T(8,128)(2,1)} %g_ref.1), custom_call_target="tpu_custom_call" | custom-call | tf_op jit(solution)/shard_map/exchange/pallas_call | solution.py:294
  100.1 16.3 %digest.1 = f32[12288,128]{1,0:T(8,128)S(1)} custom-call(s32[4,4]{1,0:T(4,128)S(1)} %copy-done.4, bf16[12288,128]{1,0:T(8,128)(2,1)S(1)} %bitcast.2, bf16[4,1024,1024]{2,1,0:T(8,128)(2,1)} %g_ref.1, bf16[4,1024,1024]{2,1,0:T(8,128)(2,1)} %get-tuple-element.11.ps_ref, bf16[4,1024,1024]{2,1,0:T(8,128)(2,1)} %get-tuple-element.12.rs_ref), custom_call_target="tpu_custom_call" | custom-call | tf_op jit(solution)/shard_map/digest/pallas_call | solution.py:404
  116.4 0.5 convert_element_type.6
  116.9 88.1 %all_to_all.5 = f16[256,48,128]{2,1,0:T(8,128)(2,1)S(1)} all-to-all(f16[256,48,128]{2,1,0:T(8,128)(2,1)S(1)} %bitcast.3), channel_id=1, replica_groups=mesh['quartet'=128,'pert'=2] {'quartet','pert'}, dimensions={0} | all-to-all | bytes 6291456 | tf_op jit(solution)/shard_map/all_to_all | solution.py:496
  205.0 0.0 copy-start.1
  205.0 0.0 copy-start.3
  205.0 0.5 convert_element_type.7.recv_ref
  205.5 0.5 copy-done.1
  206.0 0.3 copy-done.3
  206.4 8.3 %finish.1 = f32[512,256]{1,0:T(8,128)} custom-call(s32[6,256]{1,0:T(8,128)S(1)} %get-tuple-element.9.index_ref, f32[256,48,128]{2,1,0:T(8,128)S(1)} %convert_element_type.7.recv_ref, bf16[2048,256]{1,0:T(8,128)(2,1)S(1)} %copy-done.3, bf16[512,512]{1,0:T(8,128)(2,1)S(1)} %copy-done.1), custom_call_target="tpu_custom_call" | custom-call | tf_op jit(solution)/shard_map/finish/pallas_call | solution.py:474
Async XLA Ops:
  0.0 1.0 copy-start
  1.0 1.6 copy-start.2
  2.6 0.7 copy-start.4
  205.0 1.0 copy-start.1
  205.0 1.4 copy-start.3

commit v5 on v4

v5 whole, which is shorter than its diff:
```python
import jax
import jax.numpy as jnp
import numpy as np
from jax import lax
from jax.experimental import pallas as pl
from jax.experimental.pallas import tpu as pltpu
from jax.sharding import PartitionSpec as P

P_SIZE = 64
S = 32
NB = 64
QUARTERS = 4
PARTS = ((2, 3, 4, 5), (0, 1))
SPAN = NB // QUARTERS
GROUP = 4
SLOTS = 6
TILES = ((0, 1), (0, 2), (1, 3), (1, 2), (2, 3), (0, 3))
LANES = 128
SUB = 8
AREA = S * S
CHUNK = SLOTS * SUB
SCALE = 32.0

MESH = pl.DeviceIdType.MESH
EXCHANGE_VMEM = 54 << 20

f32 = jnp.float32
bf16 = jnp.bfloat16
f16 = jnp.float16


def group_swap():
    eye = np.eye(4 * LANES, dtype=np.float32)
    return jnp.asarray(eye.reshape(4, 4, S, 4 * LANES).transpose(1, 0, 2, 3).reshape(eye.shape), bf16)


def times(left, right):
    return jnp.dot(left, right, preferred_element_type=f32)


def times_turned(left, right):
    return lax.dot_general(left, right, (((1,), (1,)), ((), ())), preferred_element_type=f32)


def own_indices(quartet_ref, row_ref):
    members = [[quartet_ref[m, role] for role in range(4)] for m in range(GROUP)]
    for quarter in range(QUARTERS):
        low = quarter * SPAN

        def pick(row, column):
            total = jnp.int32(0)
            for member in members:
                within = jnp.logical_and(member[row] >= low, member[row] < low + SPAN)
                value = member[column] * SPAN + member[row] - low
                total = total + jnp.where(within, value, 0)
            return total

        for slot, (row, column) in enumerate(TILES):
            row_ref[0, 0, quarter * SLOTS + slot] = pick(row, column)
    for lane in range(QUARTERS * SLOTS, LANES):
        row_ref[0, 0, lane] = jnp.int32(0)


def exchange_kernel(
    quartet_ref,
    dens_from,
    swap_from,
    g_from,
    slots_ref,
    out_ref,
    row_ref,
    index_ref,
    lists_ref,
    dens_ref,
    swap_ref,
    message_ref,
    first_ref,
    last_ref,
    tiles_ref,
    g_ref,
    ps_ref,
    rs_ref,
    strip_ref,
    one_ref,
    two_ref,
    step_send,
    step_recv,
    own_sem,
    send_sem,
    recv_sem,
    store_sem,
):
    parts_ref = (first_ref, last_ref)
    chip, core = lax.axis_index("quartet"), lax.axis_index("pert")
    x, y, z = chip % 4, (chip // 4) % 4, chip // 16
    me = 2 * chip + core
    devices = lists_ref.shape[0]

    steps = (
        (me, 1, [(chip, (core + 1) % 2)]),
        (2 * chip, 2, [(chip - x + (x + n) % 4, core) for n in range(1, 4)]),
        (8 * (chip // 4), 8, [(chip - 4 * y + 4 * ((y + n) % 4), core) for n in range(1, 4)]),
        (32 * z, 32, [(chip - 16 * z + 16 * ((z + n) % 8), core) for n in range(1, 8)]),
    )
    barrier = pltpu.get_barrier_semaphore()
    for _, _, partners in steps:
        for partner in partners:
            pl.semaphore_signal(barrier, inc=1, device_id=partner, device_id_type=MESH)
    fetches = (
        pltpu.make_async_copy(dens_from, dens_ref, own_sem.at[1]),
        pltpu.make_async_copy(swap_from, swap_ref, own_sem.at[2]),
    )
    for fetch in fetches:
        fetch.start()
    g_load = pltpu.make_async_copy(g_from, g_ref, own_sem.at[3])
    own_indices(quartet_ref, row_ref)
    own = pltpu.make_async_copy(row_ref, lists_ref.at[pl.ds(me, 1)], own_sem.at[0])
    own.start()

    tall = dens_ref.shape[0]
    wide = dens_ref.shape[1] // LANES // len(steps)

    def cut(n):
        parts = []
        for w in range(wide):
            columns = slice(LANES * (wide * n + w), LANES * (wide * n + w + 1))
            one_ref[tall * w : tall * (w + 1), :] = dens_ref[:, columns].astype(f32)
            parts.append(
                jnp.concatenate(
                    [
                        one_ref[pl.ds(tall * w + s, LANES, stride=4), :].astype(bf16)
                        for s in range(4)
                    ],
                    axis=1,
                )
            )
        out = times(jnp.concatenate(parts, axis=0), swap_ref[...])
        for w in range(wide):
            for b in range(4):
                first = (4 * (wide * n + w) + b) * SPAN
                tiles_ref[first : first + SPAN] = out[
                    LANES * w : LANES * (w + 1), LANES * b : LANES * (b + 1)
                ].reshape(SPAN, SUB, LANES)

    own.wait()
    pl.semaphore_wait(barrier, sum(len(partners) for _, _, partners in steps))
    for n, (first, count, partners) in enumerate(steps):
        block = lists_ref.at[pl.ds(first, count)]
        for partner in partners:
            pltpu.make_async_remote_copy(
                src_ref=block,
                dst_ref=block,
                send_sem=step_send.at[n],
                recv_sem=step_recv.at[n],
                device_id=partner,
                device_id_type=MESH,
            ).start()
        if n == 0:
            for fetch in fetches:
                fetch.wait()
        cut(n)
        bytes_in = lists_ref.at[pl.ds(0, count * len(partners))]
        pltpu.make_async_copy(bytes_in, bytes_in, step_recv.at[n]).wait()

    to_scalars = pltpu.make_async_copy(lists_ref, index_ref, own_sem.at[0])
    to_scalars.start()
    g_load.start()
    to_scalars.wait()

    base = (me % QUARTERS) * SLOTS

    def pick(device, slots):
        for slot in slots[::2]:
            tiles = [tiles_ref[index_ref[device, 0, base + slot + half]] for half in range(2)]
            message_ref[device, SUB * slot : SUB * (slot + 2), :] = jnp.concatenate(
                tiles, axis=0
            ).astype(bf16)

    def send_part(part):
        slots = PARTS[part]
        rows = pl.ds(SUB * slots[0], SUB * len(slots))

        def send(n, carry):
            device = (me + n) % devices
            pick(device, slots)
            pltpu.make_async_remote_copy(
                src_ref=message_ref.at[device, rows],
                dst_ref=parts_ref[part].at[me],
                send_sem=send_sem.at[part],
                recv_sem=recv_sem.at[part],
                device_id=(device // 2, device % 2),
                device_id_type=MESH,
            ).start()
            return carry

        lax.fori_loop(1, devices, send, 0)
        pick(me, slots)
        pltpu.make_async_copy(
            message_ref.at[me, rows], parts_ref[part].at[me], own_sem.at[1 + part]
        ).start()

    for part in range(len(PARTS)):
        send_part(part)

    by_lane = lists_ref[...].reshape(devices, LANES).T
    slots = by_lane[:SLOTS]
    for quarter in range(1, QUARTERS):
        mine = by_lane[quarter * SLOTS : (quarter + 1) * SLOTS]
        slots = jnp.where(me % QUARTERS == quarter, mine, slots)
    slots_ref[...] = slots

    g_load.wait()
    count, area = g_ref.shape[0], g_ref.shape[1]
    strips = area // LANES
    gap = S + 1

    def strip(n, carry):
        m, step = n // strips, n % strips
        lanes = pl.ds(pl.multiple_of(step * LANES, LANES), LANES)
        swap = swap_ref[...]
        blocks = [g_ref[m, S * p : S * (p + 1), lanes] for p in range(S)]
        for p in range(S):
            strip_ref[gap * p : gap * p + S, :] = blocks[p].astype(f32)

        def spread(parts, target):
            out = times(jnp.concatenate(parts, axis=1), swap)
            for big in range(strips):
                for s in range(4):
                    first = gap * S * big + 4 * step + s
                    target[pl.ds(first, S, stride=gap), :] = out[
                        S * big : S * (big + 1), LANES * s : LANES * (s + 1)
                    ]

        spread(
            [
                jnp.concatenate(
                    [strip_ref[pl.ds(4 * big + r, S, stride=gap), :] for big in range(strips)],
                    axis=0,
                ).astype(bf16)
                for r in range(4)
            ],
            one_ref,
        )
        spread(
            [
                jnp.concatenate([blocks[4 * big + p] for big in range(strips)], axis=0)
                for p in range(4)
            ],
            two_ref,
        )

        @pl.when(step == strips - 1)
        def _():
            def close_up(big, carry):
                lanes = pl.ds(pl.multiple_of(big * LANES, LANES), LANES)
                for row in range(S):
                    first = gap * S * big + gap * row
                    rows = slice(S * row, S * (row + 1))
                    ps_ref[m, rows, lanes] = one_ref[pl.ds(first, S), :].astype(bf16)
                    rs_ref[m, rows, lanes] = two_ref[pl.ds(first, S), :].astype(bf16)
                return carry

            lax.fori_loop(0, strips, close_up, 0)

        return carry

    lax.fori_loop(0, count * strips, strip, 0)

    message = QUARTERS * CHUNK
    stride = message + 1
    quarters = [[quartet_ref[m, role] // SPAN for role in range(3)] for m in range(GROUP)]

    def arrive(part):
        rows = pl.ds(SUB * PARTS[part][0], SUB * len(PARTS[part]))
        pltpu.make_async_copy(
            message_ref.at[me, rows], parts_ref[part].at[me], own_sem.at[1 + part]
        ).wait()
        others = parts_ref[part].at[pl.ds(0, devices - 1)]
        pltpu.make_async_copy(others, others, recv_sem.at[part]).wait()

        def widen(pert, carry):
            for m in range(GROUP):
                for n, slot in enumerate(PARTS[part]):
                    device = QUARTERS * pert + quarters[m][TILES[slot][0]]
                    at = pert * stride + m * CHUNK + slot * SUB
                    one_ref[pl.ds(at, SUB), :] = parts_ref[part][
                        device, SUB * n : SUB * (n + 1), :
                    ].astype(f32)
            return carry

        lax.fori_loop(0, P_SIZE, widen, 0)

    def fetch_tiles(m, slot):
        first = m * CHUNK + slot * SUB
        return jnp.concatenate(
            [
                one_ref[pl.ds(first + c, P_SIZE, stride=stride), :].astype(bf16)
                for c in range(SUB)
            ],
            axis=1,
        )

    def put(m, slot, value):
        first = m * CHUNK + slot * SUB
        for c in range(SUB):
            two_ref[pl.ds(first + c, P_SIZE, stride=stride), :] = value[
                :, LANES * c : LANES * (c + 1)
            ]

    half = -0.5 * SCALE

    def first_products(m, carry):
        put(m, 1, half * times_turned(fetch_tiles(m, 2), ps_ref[m]))
        put(m, 5, half * times(fetch_tiles(m, 3), rs_ref[m]))
        put(m, 0, SCALE * times_turned(fetch_tiles(m, 4), g_ref[m]))
        put(m, 3, half * times_turned(fetch_tiles(m, 5), rs_ref[m]))
        return carry

    def last_products(m, carry):
        put(m, 4, SCALE * times(fetch_tiles(m, 0), g_ref[m]))
        put(m, 2, half * times(fetch_tiles(m, 1), ps_ref[m]))
        return carry

    arrive(0)
    lax.fori_loop(0, count, first_products, 0)
    arrive(1)
    lax.fori_loop(0, count, last_products, 0)

    def close_up(pert, carry):
        to = pl.multiple_of(pert * message, message)
        one_ref[pl.ds(to, message), :] = two_ref[pl.ds(pert * stride, message), :]
        return carry

    leaves = []
    share = P_SIZE // store_sem.shape[0]
    for n in range(store_sem.shape[0]):
        lax.fori_loop(n * share, (n + 1) * share, close_up, 0)
        rows = pl.ds(n * share * message, share * message)
        leaves.append(pltpu.make_async_copy(one_ref.at[rows], out_ref.at[rows], store_sem.at[n]))
        leaves[n].start()
    for leave in leaves:
        leave.wait()

    for part in range(len(PARTS)):
        others = parts_ref[part].at[pl.ds(0, devices - 1)]
        pltpu.make_async_copy(others, others, send_sem.at[part]).wait()
    for n, (_, count, partners) in enumerate(steps):
        bytes_out = lists_ref.at[pl.ds(0, count * len(partners))]
        pltpu.make_async_copy(bytes_out, bytes_out, step_send.at[n]).wait()


def exchange(quartets, density, swap, integrals, devices):
    whole = pl.BlockSpec(memory_space=pltpu.VMEM)
    far = pl.BlockSpec(memory_space=pltpu.HBM)
    dma = pltpu.SemaphoreType.DMA
    spaced = pltpu.VMEM((devices * CHUNK + P_SIZE, LANES), f32)
    return pl.pallas_call(
        exchange_kernel,
        in_specs=[pl.BlockSpec(memory_space=pltpu.SMEM), far, far, far],
        out_specs=[whole, far],
        out_shape=[
            jax.ShapeDtypeStruct((SLOTS, devices), jnp.int32),
            jax.ShapeDtypeStruct((devices * CHUNK, LANES), f32),
        ],
        scratch_shapes=[
            pltpu.SMEM((1, 1, LANES), jnp.int32),
            pltpu.SMEM((devices, 1, LANES), jnp.int32),
            pltpu.VMEM((devices, 1, LANES), jnp.int32),
            pltpu.VMEM(density.shape, bf16),
            pltpu.VMEM(swap.shape, bf16),
            pltpu.VMEM((devices, CHUNK, LANES), bf16),
            pltpu.VMEM((devices, SUB * len(PARTS[0]), LANES), bf16),
            pltpu.VMEM((devices, SUB * len(PARTS[1]), LANES), bf16),
            pltpu.VMEM((NB * SPAN, SUB, LANES), f32),
            pltpu.VMEM(integrals.shape, bf16),
            pltpu.VMEM(integrals.shape, bf16),
            pltpu.VMEM(integrals.shape, bf16),
            pltpu.VMEM((S * (S + 1), LANES), f32),
            spaced,
            spaced,
            dma((4,)),
            dma((4,)),
            dma((4,)),
            dma((2,)),
            dma((2,)),
            dma((8,)),
        ],
        compiler_params=pltpu.CompilerParams(
            collective_id=0, has_side_effects=True, vmem_limit_bytes=EXCHANGE_VMEM
        ),
        name="exchange",
    )(quartets, density, swap, integrals)


def order_kernel(quartet_ref, made_ref, out_ref):
    message = QUARTERS * CHUNK
    first = pl.program_id(0) * (made_ref.shape[0] // message)
    quarters = [[quartet_ref[m, role] // SPAN for role in range(3)] for m in range(GROUP)]

    def one(pert, carry):
        for m in range(GROUP):
            for slot in range(SLOTS):
                quarter = quarters[m][TILES[slot][0]]
                to = (first + pert) * message + quarter * CHUNK + slot * SUB
                to = pl.multiple_of(to, SUB)
                at = pl.multiple_of(pert * message + m * CHUNK + slot * SUB, SUB)
                out_ref[pl.ds(to, SUB), :] = made_ref[pl.ds(at, SUB), :]
        return carry

    lax.fori_loop(0, made_ref.shape[0] // message, one, 0)


def by_owner(quartets, made):
    block = pl.BlockSpec((8 * QUARTERS * CHUNK, LANES), lambda i, quartets: (i, 0))
    return pl.pallas_call(
        order_kernel,
        grid_spec=pltpu.PrefetchScalarGridSpec(
            num_scalar_prefetch=1,
            grid=(P_SIZE // 8,),
            in_specs=[block],
            out_specs=pl.BlockSpec(memory_space=pltpu.VMEM),
        ),
        out_shape=jax.ShapeDtypeStruct(made.shape, f32),
        compiler_params=pltpu.CompilerParams(vmem_limit_bytes=46 << 20),
        name="by_owner",
    )(quartets, made)


def finish_kernel(index_ref, recv_ref, orb_ref, swap_ref, out_ref, sums_ref, rows_ref, fock_ref):
    chains = sums_ref.shape[0]

    def clear(n, carry):
        sums_ref[:, pl.ds(SPAN * n, SPAN)] = jnp.zeros((chains, SPAN, SUB, LANES), f32)
        return carry

    lax.fori_loop(0, NB, clear, 0)

    def one(e, carry):
        for turn in range(SLOTS // chains):
            slots = range(turn * chains, (turn + 1) * chains)
            at = [index_ref[slot, e] for slot in slots]
            new = [
                sums_ref[chain, at[chain]] + recv_ref[e, SUB * slot : SUB * (slot + 1), :]
                for chain, slot in enumerate(slots)
            ]
            for chain in range(chains):
                sums_ref[chain, at[chain]] = new[chain]
        return carry

    lax.fori_loop(0, recv_ref.shape[0], one, 0, unroll=4)

    wide = rows_ref.shape[0]

    def columns(c, carry):
        lefts = []
        for w in range(wide):
            parts = []
            for b in range(4):
                tiles = pl.ds((4 * (wide * c + w) + b) * SPAN, SPAN)
                total = sums_ref[0, tiles]
                for chain in range(1, chains):
                    total = total + sums_ref[chain, tiles]
                parts.append((total * (1.0 / SCALE)).astype(bf16).reshape(SPAN * SUB, LANES))
            lefts.append(jnp.concatenate(parts, axis=1))
        out = times(jnp.concatenate(lefts, axis=0), swap_ref[...])
        for w in range(wide):
            for s in range(4):
                rows_ref[w, pl.ds(s, LANES, stride=4), :] = out[
                    LANES * w : LANES * (w + 1), LANES * s : LANES * (s + 1)
                ]
            at = pl.multiple_of((wide * c + w) * LANES, LANES)
            fock_ref[:, pl.ds(at, LANES)] = rows_ref[w].astype(bf16)
        return carry

    lax.fori_loop(0, NB // 4 // wide, columns, 0)
    out_ref[...] = times(fock_ref[...], orb_ref[...])


def finish(index, arrived, orbitals, swap, rows):
    basis, occupied = orbitals.shape
    chains = 3
    whole = pl.BlockSpec(memory_space=pltpu.VMEM)
    return pl.pallas_call(
        finish_kernel,
        in_specs=[pl.BlockSpec(memory_space=pltpu.SMEM), whole, whole, whole],
        out_specs=whole,
        scratch_shapes=[
            pltpu.VMEM((chains, NB * SPAN, SUB, LANES), f32),
            pltpu.VMEM((4, rows, LANES), f32),
            pltpu.VMEM((rows, basis), bf16),
        ],
        out_shape=jax.ShapeDtypeStruct((rows, occupied), f32),
        compiler_params=pltpu.CompilerParams(vmem_limit_bytes=32 << 20),
        name="finish",
    )(index, arrived, orbitals, swap)


def per_device(integrals, quartets, density, orbitals):
    axes = ("quartet", "pert")
    devices = lax.axis_size("quartet") * lax.axis_size("pert")
    swap = group_swap()
    index, made = exchange(quartets, density, swap, integrals, devices)
    terms = by_owner(quartets, made)
    leaving = terms.astype(f16).reshape(devices, CHUNK, LANES)
    landed = lax.all_to_all(leaving, axes, 0, 0, tiled=True)
    return finish(index, landed.astype(f32), orbitals, swap, density.shape[0])


def solution(mesh):
    placed = (
        P(("quartet", "pert"), None, None),
        P(("quartet", "pert"), None),
        P(("quartet", "pert"), None),
        P(),
    )
    return jax.shard_map(
        per_device,
        mesh=mesh,
        in_specs=placed,
        out_specs=P(("quartet", "pert"), None),
        check_vma=False,
    )
```

time: 215 us -> 207 us (0.963)
  local copies, waits for them, and re-layouts: 4.21 us -> 0.9 us
    pallas_call x1, Pallas kernels: 16.3 us -> 6.09 us  [by_owner(): pl.pallas_call(order_kernel, grid_spec=pltpu.PrefetchScalarGridSpec(num_s...]
    pallas_call x1, Pallas kernels: 96.8 us -> 104 us  [exchange(): pl.pallas_call(exchange_kernel, in_specs=[pl.BlockSpec(memory_space=pltpu...]
    unnamed x10 -> x8, local copies, waits for them, and re-layouts: 4.21 us -> 0.9 us
where the time goes in v5:
time: 207 us
  Pallas kernels  119 us (57%)
  blocking collectives  86.5 us (42%)
    pallas_call x1, Pallas kernels, exchange(): pl.pallas_call(exchange_kernel, in_specs=[pl.BlockSpec(memory_space=pltpu...  104 us
    all_to_all x1, blocking collectives, per_device(): landed = lax.all_to_all(leaving, axes, 0, 0, tiled=True)  86.5 us
    pallas_call x1, Pallas kernels, finish(): pl.pallas_call(finish_kernel, in_specs=[pl.BlockSpec(memory_space=pltpu.S...  8.33 us
    pallas_call x1, Pallas kernels, by_owner(): pl.pallas_call(order_kernel, grid_spec=pltpu.PrefetchScalarGridSpec(num_s...  6.09 us

profile of v5, /device:TPU:1, one launch (start us, length us, event | category | flops | bytes accessed | tf_op | source)
XLA Modules:
  0.0 207.0 jit_solution(14870090746031349988)
XLA Ops:
  0.0 0.0 copy-start.3
  0.0 104.2 %exchange.1 = (s32[6,256]{1,0:T(8,128)}, f32[12288,128]{1,0:T(8,128)}) custom-call(s32[4,4]{1,0:T(4,128)} %quartet_ref.3, bf16[512,2048]{1,0:T(8,128)(2,1)} %dens_from.1, bf16[512,512]{1,0:T(8,128)(2,1)} %constant.2.clone.swap_from.swap_ref, bf16[4,1024,1024]{2,1,0:T(8,128)(2,1)} %g_from.1), custom_call_target="tpu_custom_call" | custom-call | tf_op jit(solution)/shard_map/exchange/pallas_call | solution.py:357
  104.2 0.0 copy-done.3
  104.2 6.1 %by_owner.1 = f32[12288,128]{1,0:T(8,128)S(1)} custom-call(s32[4,4]{1,0:T(4,128)S(1)} %copy-done.3, f32[12288,128]{1,0:T(8,128)} %get-tuple-element.8.made_ref), custom_call_target="tpu_custom_call" | custom-call | tf_op jit(solution)/shard_map/by_owner/pallas_call | solution.py:415
  110.3 0.5 convert_element_type.6
  110.7 86.5 %all_to_all.5 = f16[256,48,128]{2,1,0:T(8,128)(2,1)S(1)} all-to-all(f16[256,48,128]{2,1,0:T(8,128)(2,1)S(1)} %bitcast.1), channel_id=1, replica_groups=mesh['quartet'=128,'pert'=2] {'quartet','pert'}, dimensions={0} | all-to-all | bytes 6291456 | tf_op jit(solution)/shard_map/all_to_all | solution.py:505
  197.2 0.0 copy-start
  197.2 0.0 copy-start.1
  197.2 0.0 copy-start.2
  197.2 0.5 convert_element_type.7.recv_ref
  197.7 0.5 copy-done
  198.3 0.3 copy-done.1
  198.6 0.0 copy-done.2
  198.6 8.3 %finish.1 = f32[512,256]{1,0:T(8,128)} custom-call(s32[6,256]{1,0:T(8,128)S(1)} %copy-done.2, f32[256,48,128]{2,1,0:T(8,128)S(1)} %convert_element_type.7.recv_ref, bf16[2048,256]{1,0:T(8,128)(2,1)S(1)} %copy-done.1, bf16[512,512]{1,0:T(8,128)(2,1)S(1)} %copy-done), custom_call_target="tpu_custom_call" | custom-call | tf_op jit(solution)/shard_map/finish/pallas_call | solution.py:483
Async XLA Ops:
  0.0 104.2 %copy-start.3 = (s32[4,4]{1,0:T(4,128)S(1)}, s32[4,4]{1,0:T(4,128)}, u32[]{:S(2)}) copy-start(s32[4,4]{1,0:T(4,128)} %quartet_ref.3) | copy-start | bytes 196
  197.2 1.0 copy-start
  197.2 1.4 copy-start.1
  197.2 1.4 copy-start.2

commit v6 on v5

--- a/solution.py
+++ b/solution.py
@@ -394,20 +394,22 @@
 
 def order_kernel(quartet_ref, made_ref, out_ref):
     message = QUARTERS * CHUNK
-    first = pl.program_id(0) * (made_ref.shape[0] // message)
-    quarters = [[quartet_ref[m, role] // SPAN for role in range(3)] for m in range(GROUP)]
-
-    def one(pert, carry):
+    perts = made_ref.shape[0] // message
+    first = pl.program_id(0) * perts * message
+    to = [
+        [
+            pl.multiple_of(first + quartet_ref[m, role] // SPAN * CHUNK, CHUNK)
+            for role in range(3)
+        ]
+        for m in range(GROUP)
+    ]
+    for pert in range(perts):
+        made = made_ref[message * pert : message * (pert + 1), :]
         for m in range(GROUP):
             for slot in range(SLOTS):
-                quarter = quarters[m][TILES[slot][0]]
-                to = (first + pert) * message + quarter * CHUNK + slot * SUB
-                to = pl.multiple_of(to, SUB)
-                at = pl.multiple_of(pert * message + m * CHUNK + slot * SUB, SUB)
-                out_ref[pl.ds(to, SUB), :] = made_ref[pl.ds(at, SUB), :]
-        return carry
-
-    lax.fori_loop(0, made_ref.shape[0] // message, one, 0)
+                at = m * CHUNK + slot * SUB
+                rows = pl.ds(to[m][TILES[slot][0]] + (pert * message + slot * SUB), SUB)
+                out_ref[rows, :] = made[at : at + SUB]
 
 
 def by_owner(quartets, made):

time: 207 us -> 207 us (level)
  no operation moved by 1% of the time
where the time goes in v6:
time: 207 us
  Pallas kernels  119 us (57%)
  blocking collectives  86.5 us (42%)
    pallas_call x1, Pallas kernels, exchange(): pl.pallas_call(exchange_kernel, in_specs=[pl.BlockSpec(memory_space=pltpu...  104 us
    all_to_all x1, blocking collectives, per_device(): landed = lax.all_to_all(leaving, axes, 0, 0, tiled=True)  86.5 us
    pallas_call x1, Pallas kernels, finish(): pl.pallas_call(finish_kernel, in_specs=[pl.BlockSpec(memory_space=pltpu.S...  8.33 us
    pallas_call x1, Pallas kernels, by_owner(): pl.pallas_call(order_kernel, grid_spec=pltpu.PrefetchScalarGridSpec(num_s...  6.06 us

profile of v6, /device:TPU:1, one launch (start us, length us, event | category | flops | bytes accessed | tf_op | source)
XLA Modules:
  0.0 206.9 jit_solution(223814216064749952)
XLA Ops:
  0.0 0.0 copy-start.3
  0.0 104.2 %exchange.1 = (s32[6,256]{1,0:T(8,128)}, f32[12288,128]{1,0:T(8,128)}) custom-call(s32[4,4]{1,0:T(4,128)} %quartet_ref.3, bf16[512,2048]{1,0:T(8,128)(2,1)} %dens_from.1, bf16[512,512]{1,0:T(8,128)(2,1)} %constant.2.clone.swap_from.swap_ref, bf16[4,1024,1024]{2,1,0:T(8,128)(2,1)} %g_from.1), custom_call_target="tpu_custom_call" | custom-call | tf_op jit(solution)/shard_map/exchange/pallas_call | solution.py:357
  104.2 0.0 copy-done.3
  104.2 6.1 %by_owner.1 = f32[12288,128]{1,0:T(8,128)S(1)} custom-call(s32[4,4]{1,0:T(4,128)S(1)} %copy-done.3, f32[12288,128]{1,0:T(8,128)} %get-tuple-element.8.made_ref), custom_call_target="tpu_custom_call" | custom-call | tf_op jit(solution)/shard_map/by_owner/pallas_call | solution.py:417
  110.3 0.5 convert_element_type.6
  110.7 86.5 %all_to_all.5 = f16[256,48,128]{2,1,0:T(8,128)(2,1)S(1)} all-to-all(f16[256,48,128]{2,1,0:T(8,128)(2,1)S(1)} %bitcast.1), channel_id=1, replica_groups=mesh['quartet'=128,'pert'=2] {'quartet','pert'}, dimensions={0} | all-to-all | bytes 6291456 | tf_op jit(solution)/shard_map/all_to_all | solution.py:507
  197.2 0.0 copy-start
  197.2 0.0 copy-start.1
  197.2 0.0 copy-start.2
  197.2 0.5 convert_element_type.7.recv_ref
  197.7 0.5 copy-done
  198.3 0.3 copy-done.1
  198.6 0.0 copy-done.2
  198.6 8.3 %finish.1 = f32[512,256]{1,0:T(8,128)} custom-call(s32[6,256]{1,0:T(8,128)S(1)} %copy-done.2, f32[256,48,128]{2,1,0:T(8,128)S(1)} %convert_element_type.7.recv_ref, bf16[2048,256]{1,0:T(8,128)(2,1)S(1)} %copy-done.1, bf16[512,512]{1,0:T(8,128)(2,1)S(1)} %copy-done), custom_call_target="tpu_custom_call" | custom-call | tf_op jit(solution)/shard_map/finish/pallas_call | solution.py:485
Async XLA Ops:
  0.0 104.2 %copy-start.3 = (s32[4,4]{1,0:T(4,128)S(1)}, s32[4,4]{1,0:T(4,128)}, u32[]{:S(2)}) copy-start(s32[4,4]{1,0:T(4,128)} %quartet_ref.3) | copy-start | bytes 196
  197.2 1.0 copy-start
  197.2 1.4 copy-start.1
  197.2 1.4 copy-start.2

commit v7 on v5

--- a/solution.py
+++ b/solution.py
@@ -392,35 +392,42 @@
     )(quartets, density, swap, integrals)
 
 
-def order_kernel(quartet_ref, made_ref, out_ref):
+def order_kernel(quartet_ref, made_from, out_ref, made_ref, sem):
     message = QUARTERS * CHUNK
-    first = pl.program_id(0) * (made_ref.shape[0] // message)
-    quarters = [[quartet_ref[m, role] // SPAN for role in range(3)] for m in range(GROUP)]
+    shares = sem.shape[0]
+    share = P_SIZE // shares
+    loads = []
+    for n in range(shares):
+        rows = pl.ds(n * share * message, share * message)
+        loads.append(pltpu.make_async_copy(made_from.at[rows], made_ref.at[rows], sem.at[n]))
+        loads[n].start()
+    to = [[quartet_ref[m, role] // SPAN * CHUNK for role in range(3)] for m in range(GROUP)]
 
     def one(pert, carry):
+        first = pert * message
         for m in range(GROUP):
             for slot in range(SLOTS):
-                quarter = quarters[m][TILES[slot][0]]
-                to = (first + pert) * message + quarter * CHUNK + slot * SUB
-                to = pl.multiple_of(to, SUB)
-                at = pl.multiple_of(pert * message + m * CHUNK + slot * SUB, SUB)
-                out_ref[pl.ds(to, SUB), :] = made_ref[pl.ds(at, SUB), :]
-        return carry
-
-    lax.fori_loop(0, made_ref.shape[0] // message, one, 0)
+                at = pl.multiple_of(first + m * CHUNK + slot * SUB, SUB)
+                there = pl.multiple_of(first + to[m][TILES[slot][0]] + slot * SUB, SUB)
+                out_ref[pl.ds(there, SUB), :] = made_ref[pl.ds(at, SUB), :]
+        return carry
+
+    for n in range(shares):
+        loads[n].wait()
+        lax.fori_loop(n * share, (n + 1) * share, one, 0, unroll=2)
 
 
 def by_owner(quartets, made):
-    block = pl.BlockSpec((8 * QUARTERS * CHUNK, LANES), lambda i, quartets: (i, 0))
+    shares = 8
     return pl.pallas_call(
         order_kernel,
-        grid_spec=pltpu.PrefetchScalarGridSpec(
-            num_scalar_prefetch=1,
-            grid=(P_SIZE // 8,),
-            in_specs=[block],
-            out_specs=pl.BlockSpec(memory_space=pltpu.VMEM),
-        ),
+        in_specs=[
+            pl.BlockSpec(memory_space=pltpu.SMEM),
+            pl.BlockSpec(memory_space=pltpu.HBM),
+        ],
+        out_specs=pl.BlockSpec(memory_space=pltpu.VMEM),
         out_shape=jax.ShapeDtypeStruct(made.shape, f32),
+        scratch_shapes=[pltpu.VMEM(made.shape, f32), pltpu.SemaphoreType.DMA((shares,))],
         compiler_params=pltpu.CompilerParams(vmem_limit_bytes=46 << 20),
         name="by_owner",
     )(quartets, made)

time: 207 us -> 205 us (level)
  Pallas kernels: 119 us -> 116 us
    pallas_call x1, Pallas kernels: 6.09 us -> 3.5 us  [by_owner(): pl.pallas_call(order_kernel, in_specs=[pl.BlockSpec(memory_space=pltpu.SM...]
where the time goes in v7:
time: 205 us; the launch traced here: 204 us
  Pallas kernels  116 us (57%)
  blocking collectives  86.5 us (42%)
    pallas_call x1, Pallas kernels, exchange(): pl.pallas_call(exchange_kernel, in_specs=[pl.BlockSpec(memory_space=pltpu...  104 us
    all_to_all x1, blocking collectives, per_device(): landed = lax.all_to_all(leaving, axes, 0, 0, tiled=True)  86.5 us
    pallas_call x1, Pallas kernels, finish(): pl.pallas_call(finish_kernel, in_specs=[pl.BlockSpec(memory_space=pltpu.S...  8.33 us

profile of v7, /device:TPU:1, one launch (start us, length us, event | category | flops | bytes accessed | tf_op | source)
XLA Modules:
  0.0 204.4 jit_solution(2132947730422512869)
XLA Ops:
  0.0 0.0 copy-start.3
  0.0 104.2 %exchange.1 = (s32[6,256]{1,0:T(8,128)}, f32[12288,128]{1,0:T(8,128)}) custom-call(s32[4,4]{1,0:T(4,128)} %quartet_ref.3, bf16[512,2048]{1,0:T(8,128)(2,1)} %dens_from.1, bf16[512,512]{1,0:T(8,128)(2,1)} %constant.2.clone.swap_from.swap_ref, bf16[4,1024,1024]{2,1,0:T(8,128)(2,1)} %g_from.1), custom_call_target="tpu_custom_call" | custom-call | tf_op jit(solution)/shard_map/exchange/pallas_call | solution.py:357
  104.2 0.0 copy-done.3
  104.2 3.5 %by_owner.1 = f32[12288,128]{1,0:T(8,128)S(1)} custom-call(s32[4,4]{1,0:T(4,128)S(1)} %copy-done.3, f32[12288,128]{1,0:T(8,128)} %get-tuple-element.8.made_from), custom_call_target="tpu_custom_call" | custom-call | tf_op jit(solution)/shard_map/by_owner/pallas_call | solution.py:422
  107.7 0.5 convert_element_type.6
  108.2 86.5 %all_to_all.5 = f16[256,48,128]{2,1,0:T(8,128)(2,1)S(1)} all-to-all(f16[256,48,128]{2,1,0:T(8,128)(2,1)S(1)} %bitcast.1), channel_id=1, replica_groups=mesh['quartet'=128,'pert'=2] {'quartet','pert'}, dimensions={0} | all-to-all | bytes 6291456 | tf_op jit(solution)/shard_map/all_to_all | solution.py:512
  194.6 0.0 copy-start
  194.6 0.0 copy-start.1
  194.6 0.0 copy-start.2
  194.6 0.5 convert_element_type.7.recv_ref
  195.1 0.5 copy-done
  195.7 0.3 copy-done.1
  196.0 0.0 copy-done.2
  196.0 8.3 %finish.1 = f32[512,256]{1,0:T(8,128)} custom-call(s32[6,256]{1,0:T(8,128)S(1)} %copy-done.2, f32[256,48,128]{2,1,0:T(8,128)S(1)} %convert_element_type.7.recv_ref, bf16[2048,256]{1,0:T(8,128)(2,1)S(1)} %copy-done.1, bf16[512,512]{1,0:T(8,128)(2,1)S(1)} %copy-done), custom_call_target="tpu_custom_call" | custom-call | tf_op jit(solution)/shard_map/finish/pallas_call | solution.py:490
Async XLA Ops:
  0.0 104.2 %copy-start.3 = (s32[4,4]{1,0:T(4,128)S(1)}, s32[4,4]{1,0:T(4,128)}, u32[]{:S(2)}) copy-start(s32[4,4]{1,0:T(4,128)} %quartet_ref.3) | copy-start | bytes 196
  194.6 1.0 copy-start
  194.6 1.4 copy-start.1
  194.6 1.4 copy-start.2
